TPU v7x, 512 devices: a whole 4x8x8 slice. The times are simulated.
512 devices in a mesh: seq: 64 (over z, y), tp: 8 (over x, core).
Axes of the slice: x: 4, y: 8, z: 8, core: 2. Of those that a mesh axis runs over, the one named last changes fastest.
Arguments:
- queries: bfloat16 [98304, 4096], P('seq', 'tp'), may hold values from -9 to 9
- keys: bfloat16 [98304, 1024], P('seq', 'tp'), may hold values from -10 to 10
- values: bfloat16 [98304, 1024], P('seq', 'tp'), may hold values from -12 to 12
- vertical: int32 [32, 8], replicated, may hold values from 0 to 1535, as said below
- slash: int32 [32, 2], replicated, may hold values from 0 to 8, as said below
- counts: int32 [32, 2], replicated, may hold values from 1 to 8, as said below
Outputs:
- attended: bfloat16 [98304, 4096], P(('seq', 'tp'))
Inputs may be any that keep to these rules, and one draw needn't show every extreme that they name: `vertical`: each head's list holds distinct blocks and begins with block 0; slots at or past the head's count are padding. `slash`: each head's offsets are distinct and begin with 0; slots at or past the head's count are padding. Column 0 counts a head's used vertical slots (at most 8), column 1 its used slash slots (at most 2).
All inputs are finite; a program needn't handle non-finite values.
Results may differ from a plain program's by a relative error of at most 0.0033.
Values may be sent and summed in bfloat16 or wider, within the bound.
A program may use at most 64 MiB of HBM per device.

v0:
```python
import math

import jax
import jax.numpy as jnp
from jax import lax
from jax.sharding import PartitionSpec as P

HD = 128
BLK = 64
NV = 8
NS = 2
SREACH = 8


NEG_BIG = -1e30


def shifted(value, axis, by):
    length = lax.axis_size(axis)
    pairs = [(i, i + by) for i in range(length) if 0 <= i + by < length]
    return lax.ppermute(value, axis, pairs)


def per_device(queries, keys, values, vertical, slash, counts):
    tok_dev = queries.shape[0]
    heads_loc = queries.shape[1] // HD
    kv_loc = keys.shape[1] // HD
    group_size = heads_loc // kv_loc
    blocks_dev = tok_dev // BLK
    seq_pos = lax.axis_index("seq")
    tp_pos = lax.axis_index("tp")
    score_scale_factor = 1.0 / math.sqrt(HD)
    vert_lists = lax.dynamic_slice_in_dim(vertical, tp_pos * heads_loc, heads_loc, 0)
    slash_lists = lax.dynamic_slice_in_dim(slash, tp_pos * heads_loc, heads_loc, 0)
    head_counts = lax.dynamic_slice_in_dim(counts, tp_pos * heads_loc, heads_loc, 0)
    key_blocks = keys.reshape(blocks_dev, BLK, kv_loc, HD)
    value_blocks = values.reshape(blocks_dev, BLK, kv_loc, HD)
    paired = jnp.concatenate([key_blocks, value_blocks], axis=3)
    owners = vert_lists // blocks_dev
    inside = vert_lists % blocks_dev
    pair_index = jnp.arange(heads_loc, dtype=jnp.int32) // group_size
    picked = paired[inside, :, pair_index[:, None]]
    owned_mask = (owners == seq_pos)[:, :, None, None]
    owned_terms = jnp.where(owned_mask, picked.astype(jnp.float32), 0.0)
    summed = lax.psum(owned_terms, "seq")
    gathered = summed.astype(jnp.bfloat16)
    rows_tail = SREACH * BLK
    paired_rows = jnp.concatenate([keys, values], axis=1)
    prior_rows = shifted(paired_rows[tok_dev - rows_tail :], "seq", 1)
    window = jnp.concatenate([prior_rows, paired_rows], axis=0).reshape(
        SREACH + blocks_dev, BLK, 2, kv_loc, HD
    )
    window_keys = window[:, :, 0]
    window_values = window[:, :, 1]
    query_blocks = queries.reshape(blocks_dev, BLK, heads_loc, HD)
    key_offset = jnp.arange(BLK, dtype=jnp.int32)
    local_block = jnp.arange(blocks_dev, dtype=jnp.int32)
    query_pos = seq_pos * tok_dev + local_block[:, None] * BLK + key_offset[None, :]

    def per_head(head_id):
        pair_id = head_id // group_size
        query_head_index = lax.dynamic_index_in_dim(query_blocks, head_id, 2, False)
        vert_list = vert_lists[head_id]
        slash_list = slash_lists[head_id]
        vert_valid = jnp.arange(NV, dtype=jnp.int32) < head_counts[head_id, 0]
        slash_valid = jnp.arange(NS, dtype=jnp.int32) < head_counts[head_id, 1]
        head_blocks = gathered[head_id]
        vertical_line_keys = head_blocks[:, :, :HD]
        vertical_line_values = head_blocks[:, :, HD:]
        vertical_line_score = (
            jnp.einsum(
                "itp,ofp->itof",
                query_head_index,
                vertical_line_keys,
                preferred_element_type=jnp.float32,
            )
            * score_scale_factor
        )
        vert_pos = vert_list[:, None] * BLK + key_offset[None, :]
        vert_mask = vert_valid[None, None, :, None] & (
            vert_pos[None, None, :, :] <= query_pos[:, :, None, None]
        )
        global_block = seq_pos * blocks_dev + local_block[:, None] - slash_list[None, :]
        window_block = SREACH + local_block[:, None] - slash_list[None, :]
        listed = jnp.any(
            (global_block[:, :, None] == vert_list[None, None, :]) & vert_valid[None, None, :],
            axis=2,
        )
        block_mask = slash_valid[None, :] & (global_block >= 0) & jnp.logical_not(listed)
        win_keys = lax.dynamic_index_in_dim(window_keys, pair_id, 2, False)
        win_values = lax.dynamic_index_in_dim(window_values, pair_id, 2, False)
        diagonal_keys = win_keys[window_block]
        diagonal_values = win_values[window_block]
        slash_pos = global_block[:, :, None] * BLK + key_offset[None, None, :]
        slash_mask = block_mask[:, None, :, None] & (
            slash_pos[:, None, :, :] <= query_pos[:, :, None, None]
        )
        diagonal_score = (
            jnp.einsum(
                "tfx,tywx->tfyw",
                query_head_index,
                diagonal_keys,
                preferred_element_type=jnp.float32,
            )
            * score_scale_factor
        )
        vertical_line_score = jnp.where(vert_mask, vertical_line_score, NEG_BIG)
        diagonal_score = jnp.where(slash_mask, diagonal_score, NEG_BIG)
        top = jnp.maximum(
            jnp.max(vertical_line_score, axis=(2, 3)), jnp.max(diagonal_score, axis=(2, 3))
        )
        vert_prob = jnp.where(vert_mask, jnp.exp(vertical_line_score - top[:, :, None, None]), 0.0)
        slash_prob = jnp.where(slash_mask, jnp.exp(diagonal_score - top[:, :, None, None]), 0.0)
        total = jnp.sum(vert_prob, axis=(2, 3)) + jnp.sum(slash_prob, axis=(2, 3))
        vertical_line_weight = vert_prob.astype(jnp.bfloat16)
        diagonal_weight = slash_prob.astype(jnp.bfloat16)
        numerator_rows = jnp.einsum(
            "nxmr,mrc->nxc",
            vertical_line_weight,
            vertical_line_values,
            preferred_element_type=jnp.float32,
        )
        numerator_rows = numerator_rows + jnp.einsum(
            "mnzt,mztx->mnx", diagonal_weight, diagonal_values, preferred_element_type=jnp.float32
        )
        return (numerator_rows / total[:, :, None]).astype(jnp.bfloat16).reshape(tok_dev, HD)

    head_outs = lax.map(per_head, jnp.arange(heads_loc, dtype=jnp.int32))
    attended = jnp.transpose(head_outs, (1, 0, 2)).reshape(tok_dev, heads_loc * HD)
    return lax.all_to_all(attended, "tp", split_axis=0, concat_axis=1, tiled=True)


def solution(mesh):
    return jax.shard_map(
        per_device,
        mesh=mesh,
        in_specs=(P("seq", "tp"), P("seq", "tp"), P("seq", "tp"), P(), P(), P()),
        out_specs=P(("seq", "tp"), None),
        check_vma=False,
    )
```

profile of v0, /device:TPU:1, one launch (start us, length us, event | category | flops | bytes accessed | tf_op | source)
XLA Modules:
  0.0 446.4 jit_solution(16290686737337706265)
XLA Ops:
  0.0 1.1 constant_dynamic-update-slice_fusion.1
  1.2 1.1 constant_dynamic-update-slice_fusion
  2.3 0.9 copy-done.1
  3.2 4.7 %collective-permute-start = (bf16[512,256]{1,0:T(8,128)(2,1)S(1)}, bf16[512,256]{1,0:T(8,128)(2,1)}, u32[]{:S(2)}, u32[]{:S(2)}) collective-permute-start(bf16[512,256]{1,0:T(8,128)(2,1)S(1)} %slice.34), channel_id=1, source_target_pairs={{0,8},{8,16},{16,24},{24,32},{32,40},{40,48},{48,56},{56,64},{64,7... | collective-permute-start | bytes 786440 | tf_op jit(solution)/shard_map/ppermute | solution.py:21
  9.2 253.2 %all-reduce.1 = bf16[4,8,64,256]{3,2,1,0:T(8,128)(2,1)} all-reduce(f32[4,8,64,256]{3,2,1,0:T(8,128)S(1)} %convert_select_fusion), channel_id=1, replica_groups=mesh['seq'=64,'tp'=8] {'seq'}, use_global_device_ids=true, to_apply=%region_0.1 | all-reduce | flops 524288 | bytes 3145728 | tf_op jit(solution)/shard_map/psum | solution.py:45
  262.6 2.4 reshape.303
  265.0 1.6 copy.30
  266.5 1.0 pad_maximum_fusion
  267.8 2.3 fusion.53
  270.3 88.1 %while.14 = (s32[]{:T(128)}, bf16[4,1536,128]{2,1,0:T(8,128)(2,1)}, s32[4]{0:T(128)S(1)}, s32[4,2]{0,1:T(2,128)S(1)}, s32[4,8]{1,0:T(4,128)S(1)}, /*index=5*/bf1...) while((s32[]{:T(128)}, bf16[4,1536,128]{2,1,0:T(8,128)(2,1)}, ...), condition=%wide.region_7.8_spmd.clone.clone, body=%wide.region_1.7_spmd.clone.clone.sunk | while | flops 521802400 | bytes 24216224 | solution.py:128
  272.8 0.7 constant_dynamic-slice_fusion.8
  273.5 0.6 iota_compare_fusion.4
  274.1 0.6 iota_compare_fusion.5
  275.6 1.0 dynamic-slice_bitcast_fusion.2
  276.6 0.7 gather_fusion.1
  277.3 0.7 gather_fusion
  278.0 2.4 fusion.71
  280.5 3.0 fusion.72
  283.5 1.9 convolution_bitcast_fusion.2
  285.4 0.8 fusion.74
  286.2 2.8 fusion.73
  289.1 2.5 fusion.75
  291.6 0.8 bitcast_dynamic-update-slice_fusion.2
  294.9 0.7 constant_dynamic-slice_fusion.8
  295.5 0.6 iota_compare_fusion.4
  297.7 1.0 dynamic-slice_bitcast_fusion.2
  298.6 0.7 gather_fusion.1
  299.3 0.7 gather_fusion
  300.1 2.4 fusion.71
  302.5 3.0 fusion.72
  305.5 1.9 convolution_bitcast_fusion.2
  307.4 0.8 fusion.74
  308.2 2.8 fusion.73
  311.1 2.5 fusion.75
  313.6 0.8 bitcast_dynamic-update-slice_fusion.2
  316.9 0.7 constant_dynamic-slice_fusion.8
  317.6 0.6 iota_compare_fusion.4
  318.2 0.6 iota_compare_fusion.5
  319.7 1.0 dynamic-slice_bitcast_fusion.2
  320.7 0.7 gather_fusion.1
  321.4 0.7 gather_fusion
  322.1 2.4 fusion.71
  324.5 3.0 fusion.72
  327.5 1.9 convolution_bitcast_fusion.2
  329.5 0.8 fusion.74
  330.3 2.8 fusion.73
  333.1 2.5 fusion.75
  335.7 0.8 bitcast_dynamic-update-slice_fusion.2
  338.9 0.7 constant_dynamic-slice_fusion.8
  339.6 0.6 iota_compare_fusion.4
  341.7 1.0 dynamic-slice_bitcast_fusion.2
  342.7 0.7 gather_fusion.1
  343.4 0.7 gather_fusion
  344.1 2.4 fusion.71
  346.6 3.0 fusion.72
  349.6 1.9 convolution_bitcast_fusion.2
  351.5 0.8 fusion.74
  352.3 2.8 fusion.73
  355.2 2.5 fusion.75
  357.7 0.8 bitcast_dynamic-update-slice_fusion.2
  358.5 7.6 %copy.31 = bf16[1536,4,128]{2,1,0:T(4,128)(2,1)S(1)} copy(bf16[1536,4,128]{2,0,1:T(8,128)(2,1)} %bitcast.114) | data formatting | bytes 3145728 | tf_op jit(solution)/shard_map/transpose | solution.py:129
  366.1 0.6 all_to_all.14
  366.8 78.3 %all_to_all.19 = bf16[8,192,512]{2,1,0:T(8,128)(2,1)S(1)} all-to-all(bf16[8,192,512]{2,1,0:T(8,128)(2,1)S(1)} %all_to_all.14), channel_id=1, replica_groups=mesh['seq'=64,'tp'=8] {'tp'}, dimensions={0} | all-to-all | bytes 3145728 | tf_op jit(solution)/shard_map/all_to_all | solution.py:130
  445.1 1.3 copy.42
  (105 shorter events, 9.1 us)
Async XLA Ops:
  0.0 7.9 %copy-start = (s32[32,8]{0,1:T(8,128)S(1)}, s32[32,8]{0,1:T(8,128)}, u32[]{:S(2)}) copy-start(s32[32,8]{0,1:T(8,128)} %param.11) | copy-start | bytes 3076
  0.0 8.3 %copy-start.4 = (bf16[1536,128]{1,0:T(8,128)(2,1)S(1)}, bf16[1536,128]{1,0:T(8,128)(2,1)}, u32[]{:S(2)}) copy-start(bf16[1536,128]{1,0:T(8,128)(2,1)} %param.9) | copy-start | bytes 1179652
  0.0 8.3 %copy-start.3 = (bf16[1536,128]{1,0:T(8,128)(2,1)S(1)}, bf16[1536,128]{1,0:T(8,128)(2,1)}, u32[]{:S(2)}) copy-start(bf16[1536,128]{1,0:T(8,128)(2,1)} %param.10) | copy-start | bytes 1179652
  2.2 0.9 copy-start.1
  3.2 263.4 %collective-permute-start = (bf16[512,256]{1,0:T(8,128)(2,1)S(1)}, bf16[512,256]{1,0:T(8,128)(2,1)}, u32[]{:S(2)}, u32[]{:S(2)}) collective-permute-start(bf16[512,256]{1,0:T(8,128)(2,1)S(1)} %slice.34), channel_id=1, source_target_pairs={{0,8},{8,16},{16,24},{24,32},{32,40},{40,48},{48,56},{56,64},{64,7... | collective-permute-start | bytes 786440 | tf_op jit(solution)/shard_map/ppermute | solution.py:21
  9.2 253.2 %copy-start.5 = (s32[32,2]{0,1:T(2,128)S(1)}, s32[32,2]{0,1:T(2,128)}, u32[]{:S(2)}) copy-start(s32[32,2]{0,1:T(2,128)} %param.12) | copy-start | bytes 772
  9.2 253.2 %copy-start.6 = (s32[32,2]{0,1:T(2,128)S(1)}, s32[32,2]{0,1:T(2,128)}, u32[]{:S(2)}) copy-start(s32[32,2]{0,1:T(2,128)} %param.13) | copy-start | bytes 772
  264.9 1.6 copy-start.2
where the time goes:
time: 447 us; the launch traced here: 446 us
  blocking collectives  332 us (74%)
  matrix products  39.5 us (9%)
  local copies, waits for them, and re-layouts  39.2 us (9%)
  other arithmetic  23.3 us (5%)
  loops' own time  8 us (2%)
  starting transfers between devices  4.75 us (1%)
    psum x1, blocking collectives, per_device(): summed = lax.psum(owned_terms, 'seq')  253 us
    all_to_all x1, blocking collectives, per_device(): lax.all_to_all(attended, 'tp', split_axis=0, concat_axis=1, tiled=True)  78.3 us
    reduce_sum x8, other arithmetic, per_head(): total = jnp.sum(vert_prob, axis=(2, 3)) + jnp.sum(slash_prob, axis=(2, 3))  14.5 us
    dot_general x4, matrix products, per_head(): jnp.einsum('itp,ofp->itof', query_head_index, vertical_line_keys, preferr...  12 us
    dot_general x4, matrix products, per_head(): jnp.einsum('nxmr,mrc->nxc', vertical_line_weight, vertical_line_values, p...  10.1 us
    dot_general x4, matrix products, per_head(): jnp.einsum('tfx,tywx->tfyw', query_head_index, diagonal_keys, preferred_e...  9.75 us
  transfers between devices with their start and end apart: 1, of which 0 were waited for; matrix products, arithmetic and copies ran while one was open for 1% of the time, Pallas kernels for 0%

commit v1 on v0

v1 whole, which is shorter than its diff:
```python
import functools
import math

import jax
import jax.numpy as jnp
from jax import lax
from jax.experimental import pallas as pl
from jax.experimental.pallas import tpu as pltpu
from jax.sharding import PartitionSpec as P

HD = 128
BLK = 64
NV = 8
NS = 2
SREACH = 8
HALO = SREACH * BLK

BIG = 1 << 30
NEG = -1e30
EXP2_SCALE = math.log2(math.e) / math.sqrt(HD)
MESH = pl.DeviceIdType.MESH


def attend_tile(row0, tile, head, slot0, refs):
    q_ref, wk, wv, gk, gv, kpos_v, kpos_s, off_ref, seq0 = refs
    q = q_ref[pl.ds(row0, tile), pl.ds(pl.multiple_of(head * HD, HD), HD)]
    rows = lax.broadcasted_iota(jnp.int32, (tile, HD), 0) + (seq0 + row0)
    kt = (((1,), (1,)), ((), ()))
    vert_k = gk[pl.ds(slot0, NV * BLK), :]
    vert_v = gv[pl.ds(slot0, NV * BLK), :]
    sv = lax.dot_general(q, vert_k, kt, preferred_element_type=jnp.float32)
    pair = 2 * BLK
    r_i = lax.broadcasted_iota(jnp.int32, (pair, HD), 0)
    c_i = lax.broadcasted_iota(jnp.int32, (pair, HD), 1)
    straight = (r_i < BLK) == (c_i < BLK)
    off0, off1 = off_ref
    vals = []
    ss = []
    for p in range(tile // pair):
        start = row0 + p * pair + HALO
        s0 = start + off0 * -BLK
        s1 = start + off1 * -BLK
        s1b = s1 + BLK
        k2 = jnp.concatenate(
            [wk[pl.ds(s0, pair), :], wk[pl.ds(s1b, BLK), :], wk[pl.ds(s1, BLK), :]], axis=0
        )
        v2 = jnp.concatenate(
            [wv[pl.ds(s0, pair), :], wv[pl.ds(s1b, BLK), :], wv[pl.ds(s1, BLK), :]], axis=0
        )
        both = lax.dot_general(
            q[p * pair : (p + 1) * pair], k2, kt, preferred_element_type=jnp.float32
        )
        score = jnp.where(straight, both[:, :pair], both[:, pair:])
        block = (row0 + p * pair) // BLK
        kp0 = jnp.broadcast_to(kpos_s[pl.ds(block, 1), :], (BLK, HD))
        kp1 = jnp.broadcast_to(kpos_s[pl.ds(block + 1, 1), :], (BLK, HD))
        kp = jnp.concatenate([kp0, kp1], axis=0)
        ss.append(jnp.where(kp <= rows[p * pair : (p + 1) * pair], score, NEG))
        vals.append(v2)
    ss = jnp.concatenate(ss, axis=0)
    parts = []
    for k in range(NV * BLK // HD):
        kp = kpos_v[0:1, k * HD : (k + 1) * HD]
        parts.append(jnp.where(kp <= rows, sv[:, k * HD : (k + 1) * HD], NEG))
    top = ss
    for part in parts:
        top = jnp.maximum(top, part)
    top = jnp.max(top, axis=1, keepdims=True)
    ps = jnp.exp2((ss - top) * EXP2_SCALE)
    total = ps
    probs = []
    for part in parts:
        prob = jnp.exp2((part - top) * EXP2_SCALE)
        total = total + prob
        probs.append(prob.astype(jnp.bfloat16))
    total = jnp.sum(total, axis=1, keepdims=True)
    acc = jnp.dot(
        jnp.concatenate(probs, axis=1), vert_v, preferred_element_type=jnp.float32
    )
    slash_acc = []
    for p in range(tile // pair):
        w = ps[p * pair : (p + 1) * pair]
        w2 = jnp.concatenate(
            [
                jnp.where(straight, w, 0.0).astype(jnp.bfloat16),
                jnp.where(straight, 0.0, w).astype(jnp.bfloat16),
            ],
            axis=1,
        )
        slash_acc.append(jnp.dot(w2, vals[p], preferred_element_type=jnp.float32))
    acc = acc + jnp.concatenate(slash_acc, axis=0)
    return (acc / total).astype(jnp.bfloat16)


def key_positions(head, seq, blocks_dev, vert, slash, counts, kpos_v, kpos_s):
    n_vert = counts[head, 0]
    n_slash = counts[head, 1]
    lane = lax.broadcasted_iota(jnp.int32, (8, HD), 1)
    for k in range(NV // 2):
        pos = jnp.where(lane < BLK, vert[head, 2 * k], vert[head, 2 * k + 1]) * BLK + lane % BLK
        used = jnp.where(lane < BLK, 2 * k, 2 * k + 1) < n_vert
        kpos_v[:, k * HD : (k + 1) * HD] = jnp.where(used, pos, BIG)
    row = lax.broadcasted_iota(jnp.int32, (blocks_dev, HD), 0)
    col = lax.broadcasted_iota(jnp.int32, (blocks_dev, HD), 1)
    first = (row % 2 == 0) == (col < BLK)
    block = seq * blocks_dev + row - jnp.where(first, slash[head, 0], slash[head, 1])
    dead = (block < 0) | (jnp.where(first, 0, 1) >= n_slash)
    for j in range(NV):
        dead = dead | ((block == vert[head, j]) & (jnp.full_like(row, j) < n_vert))
    kpos_s[...] = jnp.where(dead, BIG, block * BLK + col % BLK)


def fused(
    nz, ny, ntp, slots,
    vert, slash, counts, q_hbm, k_hbm, v_hbm, out,
    q_ref, wk, wv, hk, hv, snd, got1k, got1v, mid, got2k, got2v, gk, gv, obuf, kpos_v, kpos_s,
    local_sem, halo_send, halo_recv, send1, recv1, send2, recv2, send3, recv3, send4, recv4,
    own_sem, out_send, out_recv,
):
    tok = q_ref.shape[0]
    heads = q_ref.shape[1] // HD
    blocks_dev = tok // BLK
    seq = lax.axis_index("seq")
    tp = lax.axis_index("tp")
    z, y = seq // ny, seq % ny
    nseq = nz * ny
    axes = ((ny, nz), (nz, ny))
    mine = ((y, z), (z, y))

    def at(side, first, second):
        return (second * ny + first if side == 0 else first * ny + second, tp)

    def local(i, src, dst):
        return pltpu.make_async_copy(src, dst, local_sem.at[i])

    copies = [
        local(0, k_hbm, wk.at[HALO:]),
        local(1, v_hbm, wv.at[HALO:]),
        local(2, q_hbm, q_ref),
    ]
    for c in copies:
        c.start()

    barrier = pltpu.get_barrier_semaphore()

    @pl.loop(1, ny)
    def _(d):
        peer = z * ny + lax.rem(y + d, ny)
        pl.semaphore_signal(barrier, inc=1, device_id=(peer, tp), device_id_type=MESH)

    @pl.loop(1, nz)
    def _(d):
        peer = lax.rem(z + d, nz) * ny + y
        pl.semaphore_signal(barrier, inc=1, device_id=(peer, tp), device_id_type=MESH)

    @pl.loop(1, ntp)
    def _(d):
        pl.semaphore_signal(
            barrier, inc=1, device_id=(seq, lax.rem(tp + d, ntp)), device_id_type=MESH
        )

    after, before = lax.rem(seq + 1, nseq), lax.rem(seq + nseq - 1, nseq)
    for peer in (after, before):
        pl.semaphore_signal(barrier, inc=1, device_id=(peer, tp), device_id_type=MESH)

    copies[0].wait()
    copies[1].wait()

    @pl.loop(0, slots)
    def _(slot):
        block = vert[tp * heads + slot // NV, slot % NV]
        row = lax.rem(block, blocks_dev) * BLK + HALO
        dst = pl.ds(pl.multiple_of(slot * BLK, BLK), BLK)
        snd[0, dst, :] = wk[pl.ds(row, BLK), :]
        snd[1, dst, :] = wv[pl.ds(row, BLK), :]

    pl.semaphore_wait(barrier, ny + nz + ntp - 3 + 2)

    halo = [
        pltpu.make_async_remote_copy(
            src_ref=w.at[tok : tok + HALO],
            dst_ref=dst,
            send_sem=halo_send.at[i],
            recv_sem=halo_recv.at[i],
            device_id=(after, tp),
            device_id_type=MESH,
        )
        for i, (w, dst) in enumerate(((wk, hk), (wv, hv)))
    ]

    got1, got2, full = (got1k, got1v), (got2k, got2v), (gk, gv)

    def spread1(side, d):
        n, me = axes[side][0], mine[side][0]
        rows = slots * BLK // n
        peer = lax.rem(me + d, n)
        return pltpu.make_async_remote_copy(
            src_ref=snd.at[side, pl.ds(pl.multiple_of(peer * rows, 16), rows), :],
            dst_ref=got1[side].at[pl.ds(pl.multiple_of(me * rows, 16), rows), :],
            send_sem=send1.at[side, d],
            recv_sem=recv1.at[side, n - d],
            device_id=at(side, peer, mine[side][1]),
            device_id_type=MESH,
        )

    def spread2(side, d):
        n1 = axes[side][0]
        n, me = axes[side][1], mine[side][1]
        rows = slots * BLK // n1 // n
        peer = lax.rem(me + d, n)
        return pltpu.make_async_remote_copy(
            src_ref=mid.at[side, pl.ds(pl.multiple_of(peer * rows, 16), rows), :],
            dst_ref=got2[side].at[pl.ds(pl.multiple_of(me * rows, 16), rows), :],
            send_sem=send2.at[side, d],
            recv_sem=recv2.at[side, n - d],
            device_id=at(side, mine[side][0], peer),
            device_id_type=MESH,
        )


    def gather2(side, d):
        n1, me1 = axes[side][0], mine[side][0]
        n, me = axes[side][1], mine[side][1]
        rows1 = slots * BLK // n1
        rows = rows1 // n
        place = pl.ds(pl.multiple_of(me1 * rows1 + me * rows, 16), rows)
        return pltpu.make_async_remote_copy(
            src_ref=full[side].at[place, :],
            dst_ref=full[side].at[place, :],
            send_sem=send3.at[side, d],
            recv_sem=recv3.at[side, n - d],
            device_id=at(side, me1, lax.rem(me + d, n)),
            device_id_type=MESH,
        )

    def gather1(side, d):
        n, me = axes[side][0], mine[side][0]
        rows = slots * BLK // n
        place = pl.ds(pl.multiple_of(me * rows, 16), rows)
        return pltpu.make_async_remote_copy(
            src_ref=full[side].at[place, :],
            dst_ref=full[side].at[place, :],
            send_sem=send4.at[side, d],
            recv_sem=recv4.at[side, n - d],
            device_id=at(side, lax.rem(me + d, n), mine[side][1]),
            device_id_type=MESH,
        )

    def owner(slot):
        block = vert[tp * heads + slot // NV, slot % NV]
        device = lax.div(block, blocks_dev)
        return lax.rem(device, ny), lax.div(device, ny)

    def each(side, axis, step):
        @pl.loop(1, axes[side][axis])
        def _(d):
            step(d)

    for side in (0, 1):
        each(side, 0, lambda d, side=side: spread1(side, d).start())
    for c in halo:
        c.start()

    for side in (0, 1):
        n, me = axes[side][0], mine[side][0]
        rows = slots * BLK // n
        here = pl.ds(pl.multiple_of(me * rows, 16), rows)
        got1[side][here, :] = snd[side, here, :]
        each(side, 0, lambda d, side=side: spread1(side, d).wait_recv())

        @pl.loop(0, rows // BLK)
        def _(k, side=side, rows=rows, me=me):
            first = owner(me * (rows // BLK) + k)[side]
            src = first * rows + k * BLK
            dst = pl.ds(pl.multiple_of(k * BLK, BLK), BLK)
            mid[side, dst, :] = got1[side][pl.ds(src, BLK), :]

        each(side, 1, lambda d, side=side: spread2(side, d).start())

    for side in (0, 1):
        n1, me1 = axes[side][0], mine[side][0]
        n, me = axes[side][1], mine[side][1]
        rows1 = slots * BLK // n1
        rows = rows1 // n
        piece = min(rows, BLK)
        here = pl.ds(pl.multiple_of(me * rows, 16), rows)
        got2[side][here, :] = mid[side, here, :]
        each(side, 1, lambda d, side=side: spread2(side, d).wait_recv())
        for k in range(rows // piece):
            slot = (me1 * rows1 + me * rows + k * piece) // BLK
            second = owner(slot)[1 - side]
            src = second * rows + k * piece
            dst = pl.ds(pl.multiple_of(me1 * rows1 + me * rows + k * piece, 16), piece)
            full[side][dst, :] = got2[side][pl.ds(src, piece), :]
        each(side, 1, lambda d, side=side: gather2(side, d).start())

    for side in (0, 1):
        each(side, 1, lambda d, side=side: gather2(side, d).wait_recv())
        each(side, 0, lambda d, side=side: gather1(side, d).start())

    for c in halo:
        c.wait_recv()
    joins = [local(3, hk, wk.at[0:HALO]), local(4, hv, wv.at[0:HALO])]
    for c in joins:
        c.start()
    copies[2].wait()
    for c in joins:
        c.wait()
    for side in (0, 1):
        each(side, 0, lambda d, side=side: gather1(side, d).wait_recv())

    nx = ntp // 2
    part = tok // ntp
    tile = 2 * part
    x, core = tp // 2, lax.rem(tp, 2)
    order = (2, 1, 3, 0) if nx == 4 else tuple(range(nx - 1, -1, -1))

    def send_out(h, j, c, target):
        src = pl.multiple_of(c * part, 16)
        cols = pl.ds(pl.multiple_of((tp * heads + h) * HD, HD), HD)
        return pltpu.make_async_remote_copy(
            src_ref=obuf.at[h, j, pl.ds(src, part), :],
            dst_ref=out.at[:, cols],
            send_sem=out_send.at[h, j, c],
            recv_sem=out_recv.at[h, tp],
            device_id=(seq, target),
            device_id_type=MESH,
        )

    def keep_out(h, j):
        src = pl.multiple_of(core * part, 16)
        cols = pl.ds(pl.multiple_of((tp * heads + h) * HD, HD), HD)
        return pltpu.make_async_copy(
            obuf.at[h, j, pl.ds(src, part), :], out.at[:, cols], own_sem.at[h]
        )

    def landed(h, source):
        cols = pl.ds(pl.multiple_of((source * heads + h) * HD, HD), HD)
        return pltpu.make_async_remote_copy(
            src_ref=obuf.at[h, 0, pl.ds(0, part), :],
            dst_ref=out.at[:, cols],
            send_sem=out_send.at[h, 0, 0],
            recv_sem=out_recv.at[h, source],
            device_id=(seq, source),
            device_id_type=MESH,
        )

    @pl.loop(0, heads)
    def _(h):
        head = tp * heads + h
        key_positions(head, seq, blocks_dev, vert, slash, counts, kpos_v, kpos_s)
        refs = (
            q_ref, wk, wv, gk, gv, kpos_v, kpos_s,
            (slash[head, 0], slash[head, 1]), seq * tok,
        )
        for j, step in enumerate(order):
            chip = lax.rem(x + step, nx)
            row0 = pl.multiple_of(chip * tile, BLK)
            slot0 = pl.multiple_of(h * (NV * BLK), BLK)
            obuf[h, j] = attend_tile(row0, tile, h, slot0, refs)
            if step:
                for c in (0, 1):
                    send_out(h, j, c, chip * 2 + c).start()
            else:
                send_out(h, j, 1 - core, chip * 2 + 1 - core).start()
                keep_out(h, j).start()

    @pl.loop(0, heads)
    def _(h):
        @pl.loop(1, ntp)
        def _(d):
            landed(h, lax.rem(tp + d, ntp)).wait_recv()

        keep_out(h, nx - 1).wait()
        for j, step in enumerate(order):
            chip = lax.rem(x + step, nx)
            if step:
                for c in (0, 1):
                    send_out(h, j, c, chip * 2 + c).wait_send()
            else:
                send_out(h, j, 1 - core, chip * 2 + 1 - core).wait_send()

    for c in halo:
        c.wait_send()
    for side in (0, 1):
        each(side, 0, lambda d, side=side: spread1(side, d).wait_send())
        each(side, 1, lambda d, side=side: spread2(side, d).wait_send())
        each(side, 1, lambda d, side=side: gather2(side, d).wait_send())
        each(side, 0, lambda d, side=side: gather1(side, d).wait_send())


def per_device(nz, ny, ntp, queries, keys, values, vertical, slash, counts):
    tok, width = queries.shape
    heads = width // HD
    slots = heads * NV
    part = tok // ntp
    nx = ntp // 2
    big = max(ny, nz)
    dma = pltpu.SemaphoreType.DMA
    bf = jnp.bfloat16
    smem = pl.BlockSpec(memory_space=pltpu.SMEM)
    hbm = pl.BlockSpec(memory_space=pl.ANY)
    return pl.pallas_call(
        functools.partial(fused, nz, ny, ntp, slots),
        out_shape=jax.ShapeDtypeStruct((part, width * ntp), bf),
        in_specs=[smem, smem, smem, hbm, hbm, hbm],
        out_specs=hbm,
        scratch_shapes=[
            pltpu.VMEM((tok, width), bf),
            pltpu.VMEM((HALO + tok, HD), bf),
            pltpu.VMEM((HALO + tok, HD), bf),
            pltpu.VMEM((HALO, HD), bf),
            pltpu.VMEM((HALO, HD), bf),
            pltpu.VMEM((2, slots * BLK, HD), bf),
            pltpu.VMEM((slots * BLK, HD), bf),
            pltpu.VMEM((slots * BLK, HD), bf),
            pltpu.VMEM((2, slots * BLK // min(ny, nz), HD), bf),
            pltpu.VMEM((slots * BLK // ny, HD), bf),
            pltpu.VMEM((slots * BLK // nz, HD), bf),
            pltpu.VMEM((slots * BLK, HD), bf),
            pltpu.VMEM((slots * BLK, HD), bf),
            pltpu.VMEM((heads, nx, 2 * part, HD), bf),
            pltpu.VMEM((8, NV * BLK), jnp.int32),
            pltpu.VMEM((tok // BLK, HD), jnp.int32),
            dma((5,)),
            dma((2,)),
            dma((2,)),
            dma((2, big)),
            dma((2, big)),
            dma((2, big)),
            dma((2, big)),
            dma((2, big)),
            dma((2, big)),
            dma((2, big)),
            dma((2, big)),
            dma((heads,)),
            dma((heads, nx, 2)),
            dma((heads, ntp)),
        ],
        compiler_params=pltpu.CompilerParams(
            collective_id=0, has_side_effects=True, vmem_limit_bytes=48 * 2**20
        ),
    )(vertical, slash, counts, queries, keys, values)


def solution(mesh):
    nseq, ntp = mesh.shape["seq"], mesh.shape["tp"]
    ny = 1 << ((nseq.bit_length() - 1 + 1) // 2)
    return jax.shard_map(
        functools.partial(per_device, nseq // ny, ny, ntp),
        mesh=mesh,
        in_specs=(P("seq", "tp"), P("seq", "tp"), P("seq", "tp"), P(), P(), P()),
        out_specs=P(("seq", "tp"), None),
        check_vma=False,
    )
```

time: 447 us -> 88 us (0.20)
  blocking collectives: 332 us -> 0 us
  Pallas kernels: 0 us -> 80.9 us
  matrix products: 39.5 us -> 0 us
  local copies, waits for them, and re-layouts: 39.2 us -> 6.82 us
  other arithmetic: 23.3 us -> 0 us
  loops' own time: 8 us -> 0 us
  starting transfers between devices: 4.75 us -> 0 us
    psum x1 -> x0, blocking collectives: 253 us -> none  [per_device(): summed = lax.psum(owned_terms, 'seq')]
    pallas_call x0 -> x1, Pallas kernels: none -> 80.9 us  [per_device(): pl.pallas_call(functools.partial(fused, nz, ny, ntp, slots), out_shape=ja...]
    all_to_all x1 -> x0, blocking collectives: 78.3 us -> none  [per_device(): lax.all_to_all(attended, 'tp', split_axis=0, concat_axis=1, tiled=True)]
    dot_general x16 -> x0, matrix products: 39.5 us -> none  [the longest x4 12 us: per_head(): jnp.einsum('itp,ofp->itof', query_head_index, vertical_line_keys, preferr...]
    reduce_sum x8 -> x0, other arithmetic: 14.5 us -> none  [per_head(): total = jnp.sum(vert_prob, axis=(2, 3)) + jnp.sum(slash_prob, axis=(2, 3))]
    another operation x1 -> x0, loops' own time: 8 us -> none  [per_device(): head_outs = lax.map(per_head, jnp.arange(heads_loc, dtype=jnp.int32))]
    transpose x1 -> x0, local copies, waits for them, and re-layouts: 7.65 us -> none  [per_device(): jnp.transpose(head_outs, (1, 0, 2)).reshape(tok_dev, heads_loc * HD)]
    gather x9 -> x0, local copies, waits for them, and re-layouts: 6.2 us -> none  [the longest x4 2.79 us: per_head(): diagonal_keys = win_keys[window_block]]
  transfers between devices with their start and end apart: 1 -> 0, of which waited for: 0 -> 0; matrix products, arithmetic and copies ran while one was open for 1% -> 0% of each run, Pallas kernels for 0% -> 0%
where the time goes in v1:
time: 88 us; the launch traced here: 87.7 us
  Pallas kernels  80.9 us (92%)
  local copies, waits for them, and re-layouts  6.82 us (8%)
    pallas_call x1, Pallas kernels, per_device(): pl.pallas_call(functools.partial(fused, nz, ny, ntp, slots), out_shape=ja...  80.9 us
    unnamed x10, local copies, waits for them, and re-layouts  6.82 us

profile of v1, /device:TPU:1, one launch (start us, length us, event | category | flops | bytes accessed | tf_op | source)
XLA Modules:
  0.0 87.7 jit_solution(11109969037056110085)
XLA Ops:
  0.0 0.8 copy.7.vert
  0.8 0.8 copy.8.slash
  1.5 0.8 copy.9.counts
  2.3 0.0 copy-start
  2.3 1.4 %copy-done = bf16[1536,512]{1,0:T(8,128)(2,1)S(1)} copy-done((bf16[1536,512]{1,0:T(8,128)(2,1)S(1)}, bf16[1536,512]{1,0:T(8,128)(2,1)}, u32[]{:S(2)}) %copy-start) | copy-done | bytes 1572888
  3.7 0.0 copy-start.1
  3.7 1.0 %copy-done.1 = bf16[1536,128]{1,0:T(8,128)(2,1)S(1)} copy-done((bf16[1536,128]{1,0:T(8,128)(2,1)S(1)}, bf16[1536,128]{1,0:T(8,128)(2,1)}, u32[]{:S(2)}) %copy-start.1) | copy-done | bytes 393240
  4.7 0.0 copy-start.2
  4.7 1.0 %copy-done.2 = bf16[1536,128]{1,0:T(8,128)(2,1)S(1)} copy-done((bf16[1536,128]{1,0:T(8,128)(2,1)S(1)}, bf16[1536,128]{1,0:T(8,128)(2,1)}, u32[]{:S(2)}) %copy-start.2) | copy-done | bytes 393240
  5.7 80.9 %shard_map.64 = bf16[192,4096]{1,0:T(8,128)(2,1)S(1)} custom-call(s32[32,8]{1,0:T(8,128)S(1)} %copy.7.vert, s32[32,2]{1,0:T(8,128)S(1)} %copy.8.slash, s32[32,2]{1,0:T(8,128)S(1)} %copy.9.counts, bf16[1536,512]{1,0:T(8,128)(2,1)S(1)} %copy-done, bf16[1536,128]{1,0:T(8,128)(2,1)S(1)} %copy-done.1, bf16[1536,128]{1,0:T(8,128)(2,1)S(1)} %copy-done.2), custom_call_target="tpu_custom_call" | custom-call | tf_op jit(solution)/shard_map/pallas_call | solution.py:403
  86.6 1.1 %copy.11 = bf16[192,4096]{1,0:T(8,128)(2,1)} copy(bf16[192,4096]{1,0:T(8,128)(2,1)S(1)} %shard_map.64) | data formatting | bytes 3145728
Async XLA Ops:
  2.3 1.4 %copy-start = (bf16[1536,512]{1,0:T(8,128)(2,1)S(1)}, bf16[1536,512]{1,0:T(8,128)(2,1)}, u32[]{:S(2)}) copy-start(bf16[1536,512]{1,0:T(8,128)(2,1)} %q_hbm.1) | copy-start | bytes 4718596
  3.7 1.0 %copy-start.1 = (bf16[1536,128]{1,0:T(8,128)(2,1)S(1)}, bf16[1536,128]{1,0:T(8,128)(2,1)}, u32[]{:S(2)}) copy-start(bf16[1536,128]{1,0:T(8,128)(2,1)} %k_hbm.1) | copy-start | bytes 1179652
  4.7 1.0 %copy-start.2 = (bf16[1536,128]{1,0:T(8,128)(2,1)S(1)}, bf16[1536,128]{1,0:T(8,128)(2,1)}, u32[]{:S(2)}) copy-start(bf16[1536,128]{1,0:T(8,128)(2,1)} %v_hbm.1) | copy-start | bytes 1179652

commit v2 on v1

v2 whole, which is shorter than its diff:
```python
import functools
import math

import jax
import jax.numpy as jnp
from jax import lax
from jax.experimental import pallas as pl
from jax.experimental.pallas import tpu as pltpu
from jax.sharding import PartitionSpec as P

HD = 128
BLK = 64
NV = 8
NS = 2
SREACH = 8
HALO = SREACH * BLK

BIG = 1 << 30
NEG = -1e30
EXP2_SCALE = math.log2(math.e) / math.sqrt(HD)
MESH = pl.DeviceIdType.MESH


def attend_tile(row0, tile, head, slot0, refs):
    q_ref, wk, wv, kv, kpos_v, kpos_s, off_ref, seq0 = refs
    q = q_ref[pl.ds(row0, tile), pl.ds(pl.multiple_of(head * HD, HD), HD)]
    rows = lax.broadcasted_iota(jnp.int32, (tile, HD), 0) + (seq0 + row0)
    kt = (((1,), (1,)), ((), ()))
    vert_k = kv[pl.ds(slot0, NV), :BLK, :].reshape(NV * BLK, HD)
    vert_v = kv[pl.ds(slot0, NV), BLK:, :].reshape(NV * BLK, HD)
    sv = lax.dot_general(q, vert_k, kt, preferred_element_type=jnp.float32)
    pair = 2 * BLK
    r_i = lax.broadcasted_iota(jnp.int32, (pair, HD), 0)
    c_i = lax.broadcasted_iota(jnp.int32, (pair, HD), 1)
    straight = (r_i < BLK) == (c_i < BLK)
    off0, off1 = off_ref
    vals = []
    ss = []
    for p in range(tile // pair):
        start = row0 + p * pair + HALO
        s0 = start + off0 * -BLK
        s1 = start + off1 * -BLK
        s1b = s1 + BLK
        k2 = jnp.concatenate(
            [wk[pl.ds(s0, pair), :], wk[pl.ds(s1b, BLK), :], wk[pl.ds(s1, BLK), :]], axis=0
        )
        v2 = jnp.concatenate(
            [wv[pl.ds(s0, pair), :], wv[pl.ds(s1b, BLK), :], wv[pl.ds(s1, BLK), :]], axis=0
        )
        both = lax.dot_general(
            q[p * pair : (p + 1) * pair], k2, kt, preferred_element_type=jnp.float32
        )
        score = jnp.where(straight, both[:, :pair], both[:, pair:])
        block = (row0 + p * pair) // BLK
        kp0 = jnp.broadcast_to(kpos_s[pl.ds(block, 1), :], (BLK, HD))
        kp1 = jnp.broadcast_to(kpos_s[pl.ds(block + 1, 1), :], (BLK, HD))
        kp = jnp.concatenate([kp0, kp1], axis=0)
        ss.append(jnp.where(kp <= rows[p * pair : (p + 1) * pair], score, NEG))
        vals.append(v2)
    ss = jnp.concatenate(ss, axis=0)
    parts = []
    for k in range(NV * BLK // HD):
        kp = kpos_v[0:1, k * HD : (k + 1) * HD]
        parts.append(jnp.where(kp <= rows, sv[:, k * HD : (k + 1) * HD], NEG))
    top = ss
    for part in parts:
        top = jnp.maximum(top, part)
    top = jnp.max(top, axis=1, keepdims=True)
    ps = jnp.exp2((ss - top) * EXP2_SCALE)
    total = ps
    probs = []
    for part in parts:
        prob = jnp.exp2((part - top) * EXP2_SCALE)
        total = total + prob
        probs.append(prob.astype(jnp.bfloat16))
    total = jnp.sum(total, axis=1, keepdims=True)
    acc = jnp.dot(
        jnp.concatenate(probs, axis=1), vert_v, preferred_element_type=jnp.float32
    )
    slash_acc = []
    for p in range(tile // pair):
        w = ps[p * pair : (p + 1) * pair]
        w2 = jnp.concatenate(
            [
                jnp.where(straight, w, 0.0).astype(jnp.bfloat16),
                jnp.where(straight, 0.0, w).astype(jnp.bfloat16),
            ],
            axis=1,
        )
        slash_acc.append(jnp.dot(w2, vals[p], preferred_element_type=jnp.float32))
    acc = acc + jnp.concatenate(slash_acc, axis=0)
    return (acc / total).astype(jnp.bfloat16)


def key_positions(head, seq, blocks_dev, vert, slash, counts, kpos_v, kpos_s):
    n_vert = counts[0, head]
    n_slash = counts[1, head]
    lane = lax.broadcasted_iota(jnp.int32, (8, HD), 1)
    for k in range(NV // 2):
        pos = jnp.where(lane < BLK, vert[2 * k, head], vert[2 * k + 1, head]) * BLK + lane % BLK
        used = jnp.where(lane < BLK, 2 * k, 2 * k + 1) < n_vert
        kpos_v[:, k * HD : (k + 1) * HD] = jnp.where(used, pos, BIG)
    row = lax.broadcasted_iota(jnp.int32, (blocks_dev, HD), 0)
    col = lax.broadcasted_iota(jnp.int32, (blocks_dev, HD), 1)
    first = (row % 2 == 0) == (col < BLK)
    block = seq * blocks_dev + row - jnp.where(first, slash[0, head], slash[1, head])
    dead = (block < 0) | (jnp.where(first, 0, 1) >= n_slash)
    for j in range(NV):
        dead = dead | ((block == vert[j, head]) & (jnp.full_like(row, j) < n_vert))
    kpos_s[...] = jnp.where(dead, BIG, block * BLK + col % BLK)


def fused(
    nz, ny, ntp, packed,
    vert, slash, counts, piece_at, second_at, pack, q_hbm, k_hbm, v_hbm, out,
    q_ref, wk, wv, hk, hv, snd, got1k, got1v, mid, got2k, got2v, col, kv,
    obuf, obox, kpos_v, kpos_s,
    local_sem, halo_send, halo_recv, send1, recv1, send2, recv2, send3, recv3, send4, recv4,
    own_sem, out_send, out_recv, place_sem,
):
    tok = q_ref.shape[0]
    heads = q_ref.shape[1] // HD
    blocks_dev = tok // BLK
    half = heads * NV // 2
    quad = NV // 2
    seq = lax.axis_index("seq")
    tp = lax.axis_index("tp")
    z, y = seq // ny, seq % ny
    nseq = nz * ny
    axes = ((ny, nz), (nz, ny))
    mine = ((y, z), (z, y))
    got1, got2 = (got1k, got1v), (got2k, got2v)

    def at(side, first, second):
        return (second * ny + first if side == 0 else first * ny + second, tp)

    def local(i, src, dst):
        return pltpu.make_async_copy(src, dst, local_sem.at[i])

    copies = [
        local(0, k_hbm, wk.at[HALO:]),
        local(1, v_hbm, wv.at[HALO:]),
        local(2, q_hbm, q_ref),
    ]
    for c in copies:
        c.start()

    barrier = pltpu.get_barrier_semaphore()

    @pl.loop(1, ny)
    def _(d):
        peer = z * ny + lax.rem(y + d, ny)
        pl.semaphore_signal(barrier, inc=1, device_id=(peer, tp), device_id_type=MESH)

    @pl.loop(1, nz)
    def _(d):
        peer = lax.rem(z + d, nz) * ny + y
        pl.semaphore_signal(barrier, inc=1, device_id=(peer, tp), device_id_type=MESH)

    @pl.loop(1, ntp)
    def _(d):
        pl.semaphore_signal(
            barrier, inc=1, device_id=(seq, lax.rem(tp + d, ntp)), device_id_type=MESH
        )

    after, before = lax.rem(seq + 1, nseq), lax.rem(seq + nseq - 1, nseq)
    for peer in (after, before):
        pl.semaphore_signal(barrier, inc=1, device_id=(peer, tp), device_id_type=MESH)

    copies[0].wait()
    copies[1].wait()

    for side in (0, 1):
        n = axes[side][0]
        piece = 2 * BLK // n

        @pl.loop(0, packed)
        def _(k, side=side, n=n, piece=piece):
            if packed < half:
                inside = pack[side, k]
            else:
                inside = pack[side * quad + k % quad, tp * heads + k // quad]
            row = inside * BLK + HALO
            rows_k = wk[pl.ds(row, BLK), :]
            rows_v = wv[pl.ds(row, BLK), :]
            for c in range(n):
                rows, at_row = (rows_k, c * piece) if c < n // 2 else (rows_v, c * piece - BLK)
                snd[side, c, k] = rows[at_row : at_row + piece]

    pl.semaphore_wait(barrier, ny + nz + ntp - 3 + 2)

    halo = [
        pltpu.make_async_remote_copy(
            src_ref=w.at[tok : tok + HALO],
            dst_ref=dst,
            send_sem=halo_send.at[i],
            recv_sem=halo_recv.at[i],
            device_id=(after, tp),
            device_id_type=MESH,
        )
        for i, (w, dst) in enumerate(((wk, hk), (wv, hv)))
    ]

    def spread1(side, d):
        n, me = axes[side][0], mine[side][0]
        peer = lax.rem(me + d, n)
        return pltpu.make_async_remote_copy(
            src_ref=snd.at[side, peer],
            dst_ref=got1[side].at[pl.ds(me * packed, packed)],
            send_sem=send1.at[side, d],
            recv_sem=recv1.at[side, n - d],
            device_id=at(side, peer, mine[side][1]),
            device_id_type=MESH,
        )

    def spread2(side, d):
        n, me = axes[side][1], mine[side][1]
        share = half // n
        peer = lax.rem(me + d, n)
        return pltpu.make_async_remote_copy(
            src_ref=mid.at[side, pl.ds(peer * share, share)],
            dst_ref=got2[side].at[pl.ds(me * share, share)],
            send_sem=send2.at[side, d],
            recv_sem=recv2.at[side, n - d],
            device_id=at(side, mine[side][0], peer),
            device_id_type=MESH,
        )

    def gather2(side, d):
        n, me = axes[side][1], mine[side][1]
        share = half // n
        place = col.at[side, pl.ds(me * share, share)]
        return pltpu.make_async_remote_copy(
            src_ref=place,
            dst_ref=place,
            send_sem=send3.at[side, d],
            recv_sem=recv3.at[side, n - d],
            device_id=at(side, mine[side][0], lax.rem(me + d, n)),
            device_id_type=MESH,
        )

    def rows_of(side):
        n, me = axes[side][0], mine[side][0]
        piece = 2 * BLK // n
        return pl.ds(pl.multiple_of(me * piece, 16), piece)

    def gather1(h, side, d):
        n, me = axes[side][0], mine[side][0]
        return pltpu.make_async_remote_copy(
            src_ref=col.at[side, pl.ds(h * quad, quad)],
            dst_ref=kv.at[pl.ds(h * NV + side * quad, quad), rows_of(side)],
            send_sem=send4.at[h, side, d],
            recv_sem=recv4.at[h, side, n - d],
            device_id=at(side, lax.rem(me + d, n), mine[side][1]),
            device_id_type=MESH,
        )

    def each(side, axis, step):
        @pl.loop(1, axes[side][axis])
        def _(d):
            step(d)

    for side in (0, 1):
        each(side, 0, lambda d, side=side: spread1(side, d).start())
    for c in halo:
        c.start()

    for side in (0, 1):
        me = mine[side][0]
        got1[side][pl.ds(me * packed, packed)] = snd[side, me]
        each(side, 0, lambda d, side=side: spread1(side, d).wait_recv())

        @pl.loop(0, half)
        def _(i, side=side):
            mid[side, i] = got1[side][piece_at[side * quad + i % quad, tp * heads + i // quad]]

        each(side, 1, lambda d, side=side: spread2(side, d).start())

    for side in (0, 1):
        n, me = axes[side][1], mine[side][1]
        share = half // n
        got2[side][pl.ds(me * share, share)] = mid[side, pl.ds(me * share, share)]
        each(side, 1, lambda d, side=side: spread2(side, d).wait_recv())
        for r in range(share):
            i = me * share + r
            second = second_at[side * quad + i % quad, tp * heads + i // quad]
            col[side, i] = got2[side][second * share + r]
        each(side, 1, lambda d, side=side: gather2(side, d).start())

    def start_head(h):
        for side in (0, 1):
            each(side, 0, lambda d, side=side: gather1(h, side, d).start())

    def own_head(h):
        for side in (0, 1):
            kv[pl.ds(h * NV + side * quad, quad), rows_of(side)] = col[side, pl.ds(h * quad, quad)]

    for side in (0, 1):
        each(side, 1, lambda d, side=side: gather2(side, d).wait_recv())
        each(side, 0, lambda d, side=side: gather1(0, side, d).start())
    start_head(1)

    for c in halo:
        c.wait_recv()
    joins = [local(3, hk, wk.at[0:HALO]), local(4, hv, wv.at[0:HALO])]
    for c in joins:
        c.start()
    copies[2].wait()
    for c in joins:
        c.wait()

    nx = ntp // 2
    part = tok // ntp
    tile = 2 * part
    x, core = tp // 2, lax.rem(tp, 2)
    order = (2, 1, 3, 0) if nx == 4 else tuple(range(nx - 1, -1, -1))

    def send_out(h, j, c, target):
        src = pl.multiple_of(c * part, 16)
        return pltpu.make_async_remote_copy(
            src_ref=obuf.at[h, j, pl.ds(src, part), :],
            dst_ref=obox.at[tp, h],
            send_sem=out_send.at[h, j, c],
            recv_sem=out_recv.at[h, tp],
            device_id=(seq, target),
            device_id_type=MESH,
        )

    def keep_out(h, j):
        src = pl.multiple_of(core * part, 16)
        cols = pl.ds(pl.multiple_of((tp * heads + h) * HD, HD), HD)
        return pltpu.make_async_copy(
            obuf.at[h, j, pl.ds(src, part), :], out.at[:, cols], own_sem.at[h]
        )

    def place_out(h, source):
        cols = pl.ds(pl.multiple_of((source * heads + h) * HD, HD), HD)
        return pltpu.make_async_copy(obox.at[source, h], out.at[:, cols], place_sem.at[source, h])

    def landed(h, source):
        return pltpu.make_async_remote_copy(
            src_ref=obuf.at[h, 0, pl.ds(0, part), :],
            dst_ref=obox.at[source, h],
            send_sem=out_send.at[h, 0, 0],
            recv_sem=out_recv.at[h, source],
            device_id=(seq, source),
            device_id_type=MESH,
        )

    @pl.loop(0, heads)
    def _(h):
        head = tp * heads + h
        key_positions(head, seq, blocks_dev, vert, slash, counts, kpos_v, kpos_s)
        own_head(h)
        for side in (0, 1):
            each(side, 0, lambda d, side=side: gather1(h, side, d).wait_recv())
        refs = (
            q_ref, wk, wv, kv, kpos_v, kpos_s,
            (slash[0, head], slash[1, head]), seq * tok,
        )
        for j, step in enumerate(order):
            chip = lax.rem(x + step, nx)
            row0 = pl.multiple_of(chip * tile, BLK)
            obuf[h, j] = attend_tile(row0, tile, h, h * NV, refs)
            if step:
                for c in (0, 1):
                    send_out(h, j, c, chip * 2 + c).start()
            else:
                send_out(h, j, 1 - core, chip * 2 + 1 - core).start()
                keep_out(h, j).start()
            if j == 0:

                @pl.when(h < heads - 2)
                def _():
                    start_head(h + 2)

    @pl.loop(0, heads)
    def _(h):
        @pl.loop(1, ntp)
        def _(d):
            source = lax.rem(tp + d, ntp)
            landed(h, source).wait_recv()
            place_out(h, source).start()

    @pl.loop(0, heads)
    def _(h):
        @pl.loop(1, ntp)
        def _(d):
            place_out(h, lax.rem(tp + d, ntp)).wait()

        keep_out(h, nx - 1).wait()
        for j, step in enumerate(order):
            chip = lax.rem(x + step, nx)
            if step:
                for c in (0, 1):
                    send_out(h, j, c, chip * 2 + c).wait_send()
            else:
                send_out(h, j, 1 - core, chip * 2 + 1 - core).wait_send()

    for c in halo:
        c.wait_send()
    for side in (0, 1):
        each(side, 0, lambda d, side=side: spread1(side, d).wait_send())
        each(side, 1, lambda d, side=side: spread2(side, d).wait_send())
        each(side, 1, lambda d, side=side: gather2(side, d).wait_send())

    @pl.loop(0, heads)
    def _(h):
        for side in (0, 1):
            each(side, 0, lambda d, side=side: gather1(h, side, d).wait_send())


def attend(nz, ny, ntp, packed, lists, tables, queries, keys, values):
    tok, width = queries.shape
    heads = width // HD
    half = heads * NV // 2
    part = tok // ntp
    nx = ntp // 2
    big = max(ny, nz)
    pieces = [2 * BLK // n for n in (ny, nz)]
    dma = pltpu.SemaphoreType.DMA
    bf = jnp.bfloat16
    smem = pl.BlockSpec(memory_space=pltpu.SMEM)
    hbm = pl.BlockSpec(memory_space=pltpu.HBM)
    return pl.pallas_call(
        functools.partial(fused, nz, ny, ntp, packed),
        out_shape=jax.ShapeDtypeStruct((part, width * ntp), bf),
        in_specs=[smem] * 6 + [hbm] * 3,
        out_specs=pl.BlockSpec(memory_space=pl.ANY),
        scratch_shapes=[
            pltpu.VMEM((tok, width), bf),
            pltpu.VMEM((HALO + tok, HD), bf),
            pltpu.VMEM((HALO + tok, HD), bf),
            pltpu.VMEM((HALO, HD), bf),
            pltpu.VMEM((HALO, HD), bf),
            pltpu.VMEM((2, big, packed, pieces[0], HD), bf),
            pltpu.VMEM((ny * packed, pieces[0], HD), bf),
            pltpu.VMEM((nz * packed, pieces[1], HD), bf),
            pltpu.VMEM((2, half, pieces[0], HD), bf),
            pltpu.VMEM((half, pieces[0], HD), bf),
            pltpu.VMEM((half, pieces[1], HD), bf),
            pltpu.VMEM((2, half, pieces[0], HD), bf),
            pltpu.VMEM((heads * NV, 2 * BLK, HD), bf),
            pltpu.VMEM((heads, nx, 2 * part, HD), bf),
            pltpu.VMEM((ntp, heads, part, HD), bf),
            pltpu.VMEM((8, NV * BLK), jnp.int32),
            pltpu.VMEM((tok // BLK, HD), jnp.int32),
            dma((5,)),
            dma((2,)),
            dma((2,)),
            dma((2, big)),
            dma((2, big)),
            dma((2, big)),
            dma((2, big)),
            dma((2, big)),
            dma((2, big)),
            dma((heads, 2, big)),
            dma((heads, 2, big)),
            dma((heads,)),
            dma((heads, nx, 2)),
            dma((heads, ntp)),
            dma((ntp, heads)),
        ],
        compiler_params=pltpu.CompilerParams(
            collective_id=0 if packed < half else 1,
            has_side_effects=True,
            vmem_limit_bytes=60 * 2**20,
        ),
    )(*lists, *tables, queries, keys, values)


FEW = 3
CODE = 32


def plan(nz, ny, heads, blocks_dev, vert, counts, few_at, all_at, second_at, inside_at, pack, few, wide, wide_n):
    groups_heads = vert.shape[1]
    seq, tp = lax.axis_index("seq"), lax.axis_index("tp")
    wide[...] = jnp.zeros_like(wide)
    wide_n[...] = jnp.zeros_like(wide_n)
    wide[:, :groups_heads] = vert[...]
    wide_n[:, :groups_heads] = jnp.broadcast_to(counts[0:1, :], (NV, groups_heads))
    block = wide[...]
    quad = NV // 2
    slot = lax.broadcasted_iota(jnp.int32, block.shape, 0)
    lane = lax.broadcasted_iota(jnp.int32, block.shape, 1)
    j, h = slot % quad, lane % heads
    order = h * quad + j

    def split(a, by):
        q = ((a.astype(jnp.float32) + 0.5) * (1.0 / by)).astype(jnp.int32)
        return q, a - q * by

    device, inside = split(block, blocks_dev)
    dev_z, dev_y = split(device, ny)
    wanted = (slot < wide_n[...]) & ((slot > 0) | (h == 0))
    owner = jnp.where(wanted, device, -1 - order)
    rank = jnp.zeros_like(block)
    for dh in range(heads):
        moved = pltpu.roll(owner, dh, 1) if dh else owner
        for dj in range(1 - quad, quad if dh else 0):
            other = pltpu.roll(moved, (NV - dj) % NV, 0) if dj else moved
            here = (h >= dh) & (j + dj >= 0) & (j + dj < quad) & (other == owner)
            rank = rank + here.astype(jnp.int32)
    first = jnp.where(slot < quad, dev_y, dev_z)
    few_at[...] = first * FEW + jnp.minimum(rank, FEW - 1)
    all_at[...] = first * (heads * quad) + order
    second_at[...] = jnp.where(slot < quad, dev_z, dev_y)
    inside_at[...] = inside
    most = jnp.max(jnp.where(lane < groups_heads, rank, 0))
    few[0] = (most < FEW).astype(jnp.int32)
    hit = wanted & (owner == seq) & (lane >= tp * heads) & (lane < tp * heads + heads)
    place = jnp.where(rank == 0, 1, jnp.where(rank == 1, CODE, CODE * CODE))
    coded = jnp.where(hit & (rank < FEW), inside * place, 0)
    for side in (0, 1):
        total = jnp.sum(jnp.where((slot < quad) == (side == 0), coded, 0))
        for k in range(FEW):
            pack[side, k] = total & (CODE - 1)
            total = total >> 5


def per_device(nz, ny, ntp, queries, keys, values, vertical, slash, counts):
    tok, width = queries.shape
    heads = width // HD
    bf_lists = (vertical.T, slash.T, counts.T)
    wide = jax.ShapeDtypeStruct((NV, HD), jnp.int32)
    smem = pl.BlockSpec(memory_space=pltpu.SMEM)
    vmem = pl.BlockSpec(memory_space=pltpu.VMEM)
    few_at, all_at, second_at, inside_at, pack, few = pl.pallas_call(
        functools.partial(plan, nz, ny, heads, tok // BLK),
        out_shape=(wide,) * 4
        + (jax.ShapeDtypeStruct((2, FEW), jnp.int32), jax.ShapeDtypeStruct((1,), jnp.int32)),
        in_specs=[vmem, vmem],
        out_specs=(vmem,) * 4 + (smem, smem),
        scratch_shapes=[pltpu.VMEM((NV, HD), jnp.int32), pltpu.VMEM((NV, HD), jnp.int32)],
    )(bf_lists[0], bf_lists[2])

    def sparse(few_at, all_at, second_at, inside_at, pack, *args):
        return attend(nz, ny, ntp, FEW, bf_lists, (few_at, second_at, pack), *args)

    def dense(few_at, all_at, second_at, inside_at, pack, *args):
        half = heads * NV // 2
        return attend(nz, ny, ntp, half, bf_lists, (all_at, second_at, inside_at), *args)

    return lax.cond(
        few[0] > 0, sparse, dense, few_at, all_at, second_at, inside_at, pack, queries, keys, values
    )


def solution(mesh):
    nseq, ntp = mesh.shape["seq"], mesh.shape["tp"]
    ny = 1 << ((nseq.bit_length() - 1 + 1) // 2)
    return jax.shard_map(
        functools.partial(per_device, nseq // ny, ny, ntp),
        mesh=mesh,
        in_specs=(P("seq", "tp"), P("seq", "tp"), P("seq", "tp"), P(), P(), P()),
        out_specs=P(("seq", "tp"), None),
        check_vma=False,
    )
```

time: 88 us -> 69.6 us (0.79)
  Pallas kernels: 80.9 us -> 67.6 us
  local copies, waits for them, and re-layouts: 6.82 us -> 1.15 us
    pallas_call x1 -> x2, Pallas kernels: 80.9 us -> 67.6 us  [the longest x1 66 us: attend(): pl.pallas_call(functools.partial(fused, nz, ny, ntp, packed), out_shape=j...]
    unnamed x10 -> x1, local copies, waits for them, and re-layouts: 6.82 us -> 1.15 us
where the time goes in v2:
time: 69.6 us; the launch traced here: 69.4 us
  Pallas kernels  67.6 us (97%)
  local copies, waits for them, and re-layouts  1.15 us (2%)
    pallas_call x1, Pallas kernels, attend(): pl.pallas_call(functools.partial(fused, nz, ny, ntp, packed), out_shape=j...  66 us
    pallas_call x1, Pallas kernels, per_device(): pl.pallas_call(functools.partial(plan, nz, ny, heads, tok // BLK), out_sh...  1.6 us

profile of v2, /device:TPU:1, one launch (start us, length us, event | category | flops | bytes accessed | tf_op | source)
XLA Modules:
  0.0 69.4 jit_solution(18217306622570853154)
XLA Ops:
  0.0 1.6 %shard_map.66 = (s32[8,128]{1,0:T(8,128)S(1)}, s32[8,128]{1,0:T(8,128)S(1)}, s32[8,128]{1,0:T(8,128)S(1)}, s32[8,128]{1,0:T(8,128)S(1)}, s32[2,3]{1,0:T(2,128)S(1)}, /*index=5*/s32[1]{0:T(128)}) custom-call(s32[8,32]{1,0:T(8,128)} %bitcast.4, s32[2,32]{1,0:T(2,128)} %bitcast.7), custom_call_target="tpu_custom_call" | custom-call | tf_op jit(solution)/shard_map/pallas_call | solution.py:529
  2.3 66.0 %conditional.1 = (bf16[192,4096]{1,0:T(8,128)(2,1)S(1)}) conditional(s32[]{:T(128)} %bitcast.2, (s32[8,32]{1,0:T(8,128)}, s32[2,32]{1,0:T(2,128)}, s32[2,32]{1,0:T(2,128)}, s32[8,128]{1,0:T(8,128)S(1)}, s32[8,128]{1,0:T(8,128)S(1)}, /*index=5*/s32[8,128]{1,0:T(8,128)S(1)}, bf16[1536,512]{1,0:T(8,128)(2,1)}, bf16[1536,128]{1,0:T(8,128)(2,1)}, ...), branch_computations={%region_0.0_spmd, %region_1.0_spmd} | conditional | bytes 8 | solution.py:545
  2.3 66.0 %branch_1_fun.1 = bf16[192,4096]{1,0:T(8,128)(2,1)S(1)} custom-call(s32[8,32]{1,0:T(8,128)} %get-tuple-element.53.vert, s32[2,32]{1,0:T(2,128)} %get-tuple-element.54.slash, s32[2,32]{1,0:T(2,128)} %get-tuple-element.55.counts, s32[8,128]{1,0:T(8,128)S(1)} %get-tuple-element.56.piece_at, s32[8,128]{1,0:T(8,128)S(1)} %get-tuple-element.57.second_at, ...), custom_call_target="tpu_custom_call" | custom-call | tf_op jit(solution)/shard_map/cond/branch_1_fun/pallas_call | solution.py:425
  68.3 1.1 %copy.12 = bf16[192,4096]{1,0:T(8,128)(2,1)} copy(bf16[192,4096]{1,0:T(8,128)(2,1)S(1)} %get-tuple-element.74) | data formatting | bytes 3145728

commit v3 on v2

--- a/solution.py
+++ b/solution.py
@@ -26,8 +26,9 @@
     q = q_ref[pl.ds(row0, tile), pl.ds(pl.multiple_of(head * HD, HD), HD)]
     rows = lax.broadcasted_iota(jnp.int32, (tile, HD), 0) + (seq0 + row0)
     kt = (((1,), (1,)), ((), ()))
-    vert_k = kv[pl.ds(slot0, NV), :BLK, :].reshape(NV * BLK, HD)
-    vert_v = kv[pl.ds(slot0, NV), BLK:, :].reshape(NV * BLK, HD)
+    rest = (NV - 1) * BLK
+    vert_k = jnp.concatenate([kv[0, :BLK], kv[pl.ds(slot0, NV - 1), :BLK].reshape(rest, HD)], axis=0)
+    vert_v = jnp.concatenate([kv[0, BLK:], kv[pl.ds(slot0, NV - 1), BLK:].reshape(rest, HD)], axis=0)
     sv = lax.dot_general(q, vert_k, kt, preferred_element_type=jnp.float32)
     pair = 2 * BLK
     r_i = lax.broadcasted_iota(jnp.int32, (pair, HD), 0)
@@ -111,21 +112,21 @@
 
 
 def fused(
-    nz, ny, ntp, packed,
-    vert, slash, counts, piece_at, second_at, pack, q_hbm, k_hbm, v_hbm, out,
+    nz, ny, ntp, slots, packed, row_packed,
+    vert, slash, counts, pack, row_pack, slot_at, starts, q_hbm, k_hbm, v_hbm, out,
     q_ref, wk, wv, hk, hv, snd, got1k, got1v, mid, got2k, got2v, col, kv,
     obuf, obox, kpos_v, kpos_s,
-    local_sem, halo_send, halo_recv, send1, recv1, send2, recv2, send3, recv3, send4, recv4,
+    local_sem, halo_send, halo_recv, send1, recv1, send2, recv2, send3, recv3,
     own_sem, out_send, out_recv, place_sem,
 ):
     tok = q_ref.shape[0]
     heads = q_ref.shape[1] // HD
     blocks_dev = tok // BLK
-    half = heads * NV // 2
+    half = slots // 2
     quad = NV // 2
     seq = lax.axis_index("seq")
     tp = lax.axis_index("tp")
-    z, y = seq // ny, seq % ny
+    z, y = seq // ny, lax.rem(seq, ny)
     nseq = nz * ny
     axes = ((ny, nz), (nz, ny))
     mine = ((y, z), (z, y))
@@ -147,18 +148,13 @@
 
     barrier = pltpu.get_barrier_semaphore()
 
-    @pl.loop(1, ny)
-    def _(d):
+    for d in range(1, ny):
         peer = z * ny + lax.rem(y + d, ny)
         pl.semaphore_signal(barrier, inc=1, device_id=(peer, tp), device_id_type=MESH)
-
-    @pl.loop(1, nz)
-    def _(d):
+    for d in range(1, nz):
         peer = lax.rem(z + d, nz) * ny + y
         pl.semaphore_signal(barrier, inc=1, device_id=(peer, tp), device_id_type=MESH)
-
-    @pl.loop(1, ntp)
-    def _(d):
+    for d in range(1, ntp):
         pl.semaphore_signal(
             barrier, inc=1, device_id=(seq, lax.rem(tp + d, ntp)), device_id_type=MESH
         )
@@ -167,6 +163,7 @@
     for peer in (after, before):
         pl.semaphore_signal(barrier, inc=1, device_id=(peer, tp), device_id_type=MESH)
 
+    kv[slots:] = jnp.zeros_like(kv[slots:])
     copies[0].wait()
     copies[1].wait()
 
@@ -176,11 +173,7 @@
 
         @pl.loop(0, packed)
         def _(k, side=side, n=n, piece=piece):
-            if packed < half:
-                inside = pack[side, k]
-            else:
-                inside = pack[side * quad + k % quad, tp * heads + k // quad]
-            row = inside * BLK + HALO
+            row = pack[side, k] * BLK + HALO
             rows_k = wk[pl.ds(row, BLK), :]
             rows_v = wv[pl.ds(row, BLK), :]
             for c in range(n):
@@ -213,92 +206,81 @@
             device_id_type=MESH,
         )
 
-    def spread2(side, d):
+    def gather2(side, d):
         n, me = axes[side][1], mine[side][1]
-        share = half // n
         peer = lax.rem(me + d, n)
         return pltpu.make_async_remote_copy(
-            src_ref=mid.at[side, pl.ds(peer * share, share)],
-            dst_ref=got2[side].at[pl.ds(me * share, share)],
+            src_ref=mid.at[side],
+            dst_ref=got2[side].at[pl.ds(me * row_packed, row_packed)],
             send_sem=send2.at[side, d],
             recv_sem=recv2.at[side, n - d],
             device_id=at(side, mine[side][0], peer),
             device_id_type=MESH,
         )
 
-    def gather2(side, d):
-        n, me = axes[side][1], mine[side][1]
-        share = half // n
-        place = col.at[side, pl.ds(me * share, share)]
-        return pltpu.make_async_remote_copy(
-            src_ref=place,
-            dst_ref=place,
-            send_sem=send3.at[side, d],
-            recv_sem=recv3.at[side, n - d],
-            device_id=at(side, mine[side][0], lax.rem(me + d, n)),
-            device_id_type=MESH,
-        )
-
     def rows_of(side):
         n, me = axes[side][0], mine[side][0]
         piece = 2 * BLK // n
         return pl.ds(pl.multiple_of(me * piece, 16), piece)
 
-    def gather1(h, side, d):
+    more = half - quad
+
+    def parts(chunk, side):
+        if chunk == 0:
+            return pl.ds(0, quad), pl.ds(side * quad, quad)
+        return pl.ds(quad, more), pl.ds(NV + side * more, more)
+
+    def gather1(chunk, side, d):
         n, me = axes[side][0], mine[side][0]
+        src, dst = parts(chunk, side)
         return pltpu.make_async_remote_copy(
-            src_ref=col.at[side, pl.ds(h * quad, quad)],
-            dst_ref=kv.at[pl.ds(h * NV + side * quad, quad), rows_of(side)],
-            send_sem=send4.at[h, side, d],
-            recv_sem=recv4.at[h, side, n - d],
+            src_ref=col.at[side, src],
+            dst_ref=kv.at[dst, rows_of(side)],
+            send_sem=send3.at[chunk, side, d],
+            recv_sem=recv3.at[chunk, side, n - d],
             device_id=at(side, lax.rem(me + d, n), mine[side][1]),
             device_id_type=MESH,
         )
 
-    def each(side, axis, step):
-        @pl.loop(1, axes[side][axis])
-        def _(d):
-            step(d)
-
-    for side in (0, 1):
-        each(side, 0, lambda d, side=side: spread1(side, d).start())
-    for c in halo:
-        c.start()
+    def far_first(n):
+        return sorted(range(1, n), key=lambda d: -min(d, n - d))
+
+    def each(axis, step):
+        for d in far_first(max(ny, nz)):
+            for side in (0, 1):
+                if d < axes[side][axis]:
+                    step(side, d)
+
+    each(0, lambda side, d: spread1(side, d).start())
+    halo[0].start()
 
     for side in (0, 1):
         me = mine[side][0]
         got1[side][pl.ds(me * packed, packed)] = snd[side, me]
-        each(side, 0, lambda d, side=side: spread1(side, d).wait_recv())
-
-        @pl.loop(0, half)
-        def _(i, side=side):
-            mid[side, i] = got1[side][piece_at[side * quad + i % quad, tp * heads + i // quad]]
-
-        each(side, 1, lambda d, side=side: spread2(side, d).start())
-
     for side in (0, 1):
-        n, me = axes[side][1], mine[side][1]
-        share = half // n
-        got2[side][pl.ds(me * share, share)] = mid[side, pl.ds(me * share, share)]
-        each(side, 1, lambda d, side=side: spread2(side, d).wait_recv())
-        for r in range(share):
-            i = me * share + r
-            second = second_at[side * quad + i % quad, tp * heads + i // quad]
-            col[side, i] = got2[side][second * share + r]
-        each(side, 1, lambda d, side=side: gather2(side, d).start())
-
-    def start_head(h):
+        for d in range(1, axes[side][0]):
+            spread1(side, d).wait_recv()
+        for k in range(row_packed):
+            mid[side, k] = got1[side][row_pack[side, k]]
+        for d in far_first(axes[side][1]):
+            gather2(side, d).start()
+    halo[1].start()
+
+    for side in (0, 1):
+        me = mine[side][1]
+        got2[side][pl.ds(me * row_packed, row_packed)] = mid[side]
+    for side in (0, 1):
+        for d in range(1, axes[side][1]):
+            gather2(side, d).wait_recv()
+        for i in range(half):
+            col[side, i] = got2[side][slot_at[side, i]]
+        for d in far_first(axes[side][0]):
+            gather1(0, side, d).start()
+    each(0, lambda side, d: gather1(1, side, d).start())
+    for chunk in (0, 1):
         for side in (0, 1):
-            each(side, 0, lambda d, side=side: gather1(h, side, d).start())
-
-    def own_head(h):
-        for side in (0, 1):
-            kv[pl.ds(h * NV + side * quad, quad), rows_of(side)] = col[side, pl.ds(h * quad, quad)]
-
-    for side in (0, 1):
-        each(side, 1, lambda d, side=side: gather2(side, d).wait_recv())
-        each(side, 0, lambda d, side=side: gather1(0, side, d).start())
-    start_head(1)
+            src, dst = parts(chunk, side)
+            kv[dst, rows_of(side)] = col[side, src]
 
     for c in halo:
         c.wait_recv()
@@ -347,13 +329,11 @@
             device_id_type=MESH,
         )
 
-    @pl.loop(0, heads)
-    def _(h):
+    def run_head(h, slot0):
         head = tp * heads + h
         key_positions(head, seq, blocks_dev, vert, slash, counts, kpos_v, kpos_s)
-        own_head(h)
-        for side in (0, 1):
-            each(side, 0, lambda d, side=side: gather1(h, side, d).wait_recv())
+        if isinstance(h, int):
+            each(0, lambda side, d: gather1(0, side, d).wait_recv())
         refs = (
             q_ref, wk, wv, kv, kpos_v, kpos_s,
             (slash[0, head], slash[1, head]), seq * tok,
@@ -361,18 +341,20 @@
         for j, step in enumerate(order):
             chip = lax.rem(x + step, nx)
             row0 = pl.multiple_of(chip * tile, BLK)
-            obuf[h, j] = attend_tile(row0, tile, h, h * NV, refs)
+            obuf[h, j] = attend_tile(row0, tile, h, slot0, refs)
             if step:
                 for c in (0, 1):
                     send_out(h, j, c, chip * 2 + c).start()
             else:
                 send_out(h, j, 1 - core, chip * 2 + 1 - core).start()
                 keep_out(h, j).start()
-            if j == 0:
-
-                @pl.when(h < heads - 2)
-                def _():
-                    start_head(h + 2)
+
+    run_head(0, 1)
+    each(0, lambda side, d: gather1(1, side, d).wait_recv())
+
+    @pl.loop(1, heads)
+    def _(h):
+        run_head(h, starts[h])
 
     @pl.loop(0, heads)
     def _(h):
@@ -399,33 +381,28 @@
 
     for c in halo:
         c.wait_send()
-    for side in (0, 1):
-        each(side, 0, lambda d, side=side: spread1(side, d).wait_send())
-        each(side, 1, lambda d, side=side: spread2(side, d).wait_send())
-        each(side, 1, lambda d, side=side: gather2(side, d).wait_send())
-
-    @pl.loop(0, heads)
-    def _(h):
-        for side in (0, 1):
-            each(side, 0, lambda d, side=side: gather1(h, side, d).wait_send())
-
-
-def attend(nz, ny, ntp, packed, lists, tables, queries, keys, values):
+    each(0, lambda side, d: spread1(side, d).wait_send())
+    each(1, lambda side, d: gather2(side, d).wait_send())
+    for chunk in (0, 1):
+        each(0, lambda side, d: gather1(chunk, side, d).wait_send())
+
+
+def attend(nz, ny, ntp, slots, packed, row_packed, lists, tables, queries, keys, values):
     tok, width = queries.shape
     heads = width // HD
-    half = heads * NV // 2
     part = tok // ntp
     nx = ntp // 2
     big = max(ny, nz)
+    half = slots // 2
     pieces = [2 * BLK // n for n in (ny, nz)]
     dma = pltpu.SemaphoreType.DMA
     bf = jnp.bfloat16
     smem = pl.BlockSpec(memory_space=pltpu.SMEM)
     hbm = pl.BlockSpec(memory_space=pltpu.HBM)
     return pl.pallas_call(
-        functools.partial(fused, nz, ny, ntp, packed),
+        functools.partial(fused, nz, ny, ntp, slots, packed, row_packed),
         out_shape=jax.ShapeDtypeStruct((part, width * ntp), bf),
-        in_specs=[smem] * 6 + [hbm] * 3,
+        in_specs=[smem] * 7 + [hbm] * 3,
         out_specs=pl.BlockSpec(memory_space=pl.ANY),
         scratch_shapes=[
             pltpu.VMEM((tok, width), bf),
@@ -436,11 +413,11 @@
             pltpu.VMEM((2, big, packed, pieces[0], HD), bf),
             pltpu.VMEM((ny * packed, pieces[0], HD), bf),
             pltpu.VMEM((nz * packed, pieces[1], HD), bf),
+            pltpu.VMEM((2, row_packed, pieces[0], HD), bf),
+            pltpu.VMEM((nz * row_packed, pieces[0], HD), bf),
+            pltpu.VMEM((ny * row_packed, pieces[1], HD), bf),
             pltpu.VMEM((2, half, pieces[0], HD), bf),
-            pltpu.VMEM((half, pieces[0], HD), bf),
-            pltpu.VMEM((half, pieces[1], HD), bf),
-            pltpu.VMEM((2, half, pieces[0], HD), bf),
-            pltpu.VMEM((heads * NV, 2 * BLK, HD), bf),
+            pltpu.VMEM((slots + NV, 2 * BLK, HD), bf),
             pltpu.VMEM((heads, nx, 2 * part, HD), bf),
             pltpu.VMEM((ntp, heads, part, HD), bf),
             pltpu.VMEM((8, NV * BLK), jnp.int32),
@@ -452,17 +429,15 @@
             dma((2, big)),
             dma((2, big)),
             dma((2, big)),
-            dma((2, big)),
-            dma((2, big)),
-            dma((heads, 2, big)),
-            dma((heads, 2, big)),
+            dma((2, 2, big)),
+            dma((2, 2, big)),
             dma((heads,)),
             dma((heads, nx, 2)),
             dma((heads, ntp)),
             dma((ntp, heads)),
         ],
         compiler_params=pltpu.CompilerParams(
-            collective_id=0 if packed < half else 1,
+            collective_id=0 if packed == FEW else 1,
             has_side_effects=True,
             vmem_limit_bytes=60 * 2**20,
         ),
@@ -470,81 +445,156 @@
 
 
 FEW = 3
-CODE = 32
-
-
-def plan(nz, ny, heads, blocks_dev, vert, counts, few_at, all_at, second_at, inside_at, pack, few, wide, wide_n):
-    groups_heads = vert.shape[1]
+FEW_ROW = 5
+FEW_SLOTS = 20
+
+
+def plan(nz, ny, heads, blocks_dev, vert, counts, vert_v, counts_v, pack, row_pack, slot_at, starts, few, wide, wide_n, listed):
+    all_heads = vert.shape[1]
     seq, tp = lax.axis_index("seq"), lax.axis_index("tp")
+    quad = NV // 2
     wide[...] = jnp.zeros_like(wide)
-    wide_n[...] = jnp.zeros_like(wide_n)
-    wide[:, :groups_heads] = vert[...]
-    wide_n[:, :groups_heads] = jnp.broadcast_to(counts[0:1, :], (NV, groups_heads))
-    block = wide[...]
-    quad = NV // 2
-    slot = lax.broadcasted_iota(jnp.int32, block.shape, 0)
-    lane = lax.broadcasted_iota(jnp.int32, block.shape, 1)
-    j, h = slot % quad, lane % heads
-    order = h * quad + j
-
-    def split(a, by):
-        q = ((a.astype(jnp.float32) + 0.5) * (1.0 / by)).astype(jnp.int32)
-        return q, a - q * by
-
-    device, inside = split(block, blocks_dev)
-    dev_z, dev_y = split(device, ny)
-    wanted = (slot < wide_n[...]) & ((slot > 0) | (h == 0))
-    owner = jnp.where(wanted, device, -1 - order)
-    rank = jnp.zeros_like(block)
+    wide_n[...] = jnp.ones_like(wide_n)
+    wide[:, :all_heads] = vert_v[...]
+    wide_n[:, :all_heads] = jnp.broadcast_to(counts_v[0:1, :], (NV, all_heads))
+    used = wide_n[...]
+    slot = lax.broadcasted_iota(jnp.int32, used.shape, 0)
+    lane = lax.broadcasted_iota(jnp.int32, used.shape, 1)
+    h = lane % heads
+
+    def whole(a, by):
+        return ((a.astype(jnp.float32) + 0.5) * (1.0 / by)).astype(jnp.int32)
+
+    device = whole(wide[...], blocks_dev)
+    at_z = whole(device, ny)
+    wanted = (slot < used) & ((slot > 0) | (h == 0))
+    before = jnp.zeros_like(used)
+    for dh in range(1, heads):
+        before = before + jnp.where(h >= dh, pltpu.roll(used - 1, dh, 1), 0)
+    position = jnp.where(slot == 0, 0, before + slot)
+    few_half = FEW_SLOTS // 2
+    late = position - NV
+    upper = jnp.where(late < 0, position - quad, late - (few_half - quad)) >= 0
+    alone = -1 - slot - NV * h
+    owner = jnp.where(wanted, device, alone)
+    row = jnp.where(wanted, jnp.where(upper, nz + device - at_z * ny, at_z), alone)
+    rank = jnp.zeros_like(owner)
+    row_rank = jnp.zeros_like(owner)
     for dh in range(heads):
         moved = pltpu.roll(owner, dh, 1) if dh else owner
-        for dj in range(1 - quad, quad if dh else 0):
-            other = pltpu.roll(moved, (NV - dj) % NV, 0) if dj else moved
-            here = (h >= dh) & (j + dj >= 0) & (j + dj < quad) & (other == owner)
-            rank = rank + here.astype(jnp.int32)
-    first = jnp.where(slot < quad, dev_y, dev_z)
-    few_at[...] = first * FEW + jnp.minimum(rank, FEW - 1)
-    all_at[...] = first * (heads * quad) + order
-    second_at[...] = jnp.where(slot < quad, dev_z, dev_y)
-    inside_at[...] = inside
-    most = jnp.max(jnp.where(lane < groups_heads, rank, 0))
-    few[0] = (most < FEW).astype(jnp.int32)
-    hit = wanted & (owner == seq) & (lane >= tp * heads) & (lane < tp * heads + heads)
-    place = jnp.where(rank == 0, 1, jnp.where(rank == 1, CODE, CODE * CODE))
-    coded = jnp.where(hit & (rank < FEW), inside * place, 0)
-    for side in (0, 1):
-        total = jnp.sum(jnp.where((slot < quad) == (side == 0), coded, 0))
-        for k in range(FEW):
-            pack[side, k] = total & (CODE - 1)
-            total = total >> 5
+        moved_row = pltpu.roll(row, dh, 1) if dh else row
+        for dj in range(1 - NV, NV if dh else 0):
+            here = (h >= dh) & (slot + dj >= 0) & (slot + dj < NV)
+            by = (NV - dj) % NV
+            other = pltpu.roll(moved, by, 0) if by else moved
+            other_row = pltpu.roll(moved_row, by, 0) if by else moved_row
+            rank = rank + (here & (other == owner)).astype(jnp.int32)
+            row_rank = row_rank + (here & (other_row == row)).astype(jnp.int32)
+    over = (rank >= FEW) | (row_rank >= FEW_ROW) | (before + used > FEW_SLOTS)
+    is_few = jnp.max(jnp.where((lane < all_heads) & over, 1, 0)) == 0
+    few[0] = is_few.astype(jnp.int32)
+
+    @pl.loop(0, heads * NV)
+    def _(p):
+        listed[p] = 0
+
+    end = jnp.int32(1)
+    for head in range(heads):
+        starts[head] = end
+        n = counts[0, tp * heads + head]
+        for j in range(1, NV):
+
+            @pl.when(j < n)
+            def _(j=j, head=head, end=end):
+                listed[end + j - 1] = vert[j, tp * heads + head]
+
+        end = end + n - 1
+
+    def split(block):
+        by = lax.div(block, blocks_dev)
+        z = lax.div(by, ny)
+        return by, z, by - z * ny
+
+    def tables(slots, packed, row_packed):
+        half = slots // 2
+        sparse = packed == FEW
+        for side in (0, 1):
+
+            def at(i, side=side):
+                return jnp.where(i < quad, side * quad + i, NV + side * (half - quad) + i - quad)
+
+            for k in range(packed):
+                pack[side, k] = 0
+            for k in range(row_packed):
+                row_pack[side, k] = 0
+
+            @pl.loop(0, half)
+            def _(i, side=side, at=at):
+                p = at(i)
+                owner, z, y = split(listed[p])
+                first, second = (y, z) if side == 0 else (z, y)
+                inside = listed[p] - owner * blocks_dev
+                my_second = lax.div(seq, ny) if side == 0 else lax.rem(seq, ny)
+                real = p < end
+
+                def count(o, c):
+                    other, oz, oy = split(listed[at(o)])
+                    same = (other == owner) & real
+                    same_row = ((oz if side == 0 else oy) == second) & real
+                    return c[0] + same.astype(jnp.int32), c[1] + same_row.astype(jnp.int32)
+
+                if sparse:
+                    place, row_place = lax.fori_loop(0, i, count, (jnp.int32(0), jnp.int32(0)))
+                else:
+                    place = row_place = i
+
+                @pl.when((owner == seq) & real)
+                def _():
+                    pack[side, place] = inside
+
+                @pl.when((second == my_second) & real)
+                def _():
+                    row_pack[side, row_place] = first * packed + place
+
+                slot_at[side, i] = second * row_packed + row_place
+
+    @pl.when(is_few)
+    def _():
+        tables(FEW_SLOTS, FEW, FEW_ROW)
+
+    @pl.when(jnp.logical_not(is_few))
+    def _():
+        tables(heads * NV, heads * NV // 2, heads * NV // 2)
 
 
 def per_device(nz, ny, ntp, queries, keys, values, vertical, slash, counts):
     tok, width = queries.shape
     heads = width // HD
-    bf_lists = (vertical.T, slash.T, counts.T)
-    wide = jax.ShapeDtypeStruct((NV, HD), jnp.int32)
+    half = heads * NV // 2
+    lists = (vertical.T, slash.T, counts.T)
+    table = jax.ShapeDtypeStruct((2, half), jnp.int32)
     smem = pl.BlockSpec(memory_space=pltpu.SMEM)
     vmem = pl.BlockSpec(memory_space=pltpu.VMEM)
-    few_at, all_at, second_at, inside_at, pack, few = pl.pallas_call(
+    *tables, few = pl.pallas_call(
         functools.partial(plan, nz, ny, heads, tok // BLK),
-        out_shape=(wide,) * 4
-        + (jax.ShapeDtypeStruct((2, FEW), jnp.int32), jax.ShapeDtypeStruct((1,), jnp.int32)),
-        in_specs=[vmem, vmem],
-        out_specs=(vmem,) * 4 + (smem, smem),
-        scratch_shapes=[pltpu.VMEM((NV, HD), jnp.int32), pltpu.VMEM((NV, HD), jnp.int32)],
-    )(bf_lists[0], bf_lists[2])
-
-    def sparse(few_at, all_at, second_at, inside_at, pack, *args):
-        return attend(nz, ny, ntp, FEW, bf_lists, (few_at, second_at, pack), *args)
-
-    def dense(few_at, all_at, second_at, inside_at, pack, *args):
-        half = heads * NV // 2
-        return attend(nz, ny, ntp, half, bf_lists, (all_at, second_at, inside_at), *args)
-
-    return lax.cond(
-        few[0] > 0, sparse, dense, few_at, all_at, second_at, inside_at, pack, queries, keys, values
-    )
+        out_shape=(table,) * 3
+        + (jax.ShapeDtypeStruct((heads,), jnp.int32), jax.ShapeDtypeStruct((1,), jnp.int32)),
+        in_specs=[smem, smem, vmem, vmem],
+        out_specs=(smem,) * 5,
+        scratch_shapes=[
+            pltpu.VMEM((NV, HD), jnp.int32),
+            pltpu.VMEM((NV, HD), jnp.int32),
+            pltpu.SMEM((heads * NV,), jnp.int32),
+        ],
+    )(lists[0], lists[2], lists[0], lists[2])
+
+    def sparse(tables, *args):
+        return attend(nz, ny, ntp, FEW_SLOTS, FEW, FEW_ROW, lists, tables, *args)
+
+    def dense(tables, *args):
+        return attend(nz, ny, ntp, heads * NV, half, half, lists, tables, *args)
+
+    return lax.cond(few[0] > 0, sparse, dense, tables, queries, keys, values)
 
 
 def solution(mesh):

time: 69.6 us -> 62.2 us (0.89)
  Pallas kernels: 67.6 us -> 60 us
    pallas_call x1, Pallas kernels: 66 us -> 55.9 us  [attend(): pl.pallas_call(functools.partial(fused, nz, ny, ntp, slots, packed, row_p...]
    pallas_call x1, Pallas kernels: 1.6 us -> 4.06 us  [per_device(): pl.pallas_call(functools.partial(plan, nz, ny, heads, tok // BLK), out_sh...]
where the time goes in v3:
time: 62.2 us; the launch traced here: 62 us
  Pallas kernels  60 us (96%)
  local copies, waits for them, and re-layouts  1.15 us (2%)
  between operations  0.67 us (1%)
    pallas_call x1, Pallas kernels, attend(): pl.pallas_call(functools.partial(fused, nz, ny, ntp, slots, packed, row_p...  55.9 us
    pallas_call x1, Pallas kernels, per_device(): pl.pallas_call(functools.partial(plan, nz, ny, heads, tok // BLK), out_sh...  4.06 us

profile of v3, /device:TPU:1, one launch (start us, length us, event | category | flops | bytes accessed | tf_op | source)
XLA Modules:
  0.0 62.0 jit_solution(513828326873989441)
XLA Ops:
  0.0 4.1 %shard_map.72 = (s32[2,16]{1,0:T(2,128)S(1)}, s32[2,16]{1,0:T(2,128)S(1)}, s32[2,16]{1,0:T(2,128)S(1)}, s32[4]{0:T(128)S(1)}, s32[1]{0:T(128)}) custom-call(s32[8,32]{1,0:T(8,128)} %bitcast.4, s32[2,32]{1,0:T(2,128)} %bitcast.8, s32[8,32]{1,0:T(8,128)} %bitcast.5, s32[2,32]{1,0:T(2,128)} %bitcast.9), custom_call_target="tpu_custom_call" | custom-call | tf_op jit(solution)/shard_map/pallas_call | solution.py:578
  4.7 56.1 %conditional.1 = (bf16[192,4096]{1,0:T(8,128)(2,1)S(1)}) conditional(s32[]{:T(128)} %bitcast.2, (s32[8,32]{1,0:T(8,128)}, s32[2,32]{1,0:T(2,128)}, s32[2,32]{1,0:T(2,128)}, s32[2,16]{1,0:T(2,128)S(1)}, s32[2,16]{1,0:T(2,128)S(1)}, /*index=5*/s32[2,16]{1,0:T(2,128)S(1)}, s32[4]{0:T(128)S(1)}, bf16[1536,512]{1,0:T(8,128)(2,1)}, ...), branch_computations={%region_0.0_spmd, %region_1.0_spmd} | conditional | bytes 8 | solution.py:597
  4.9 55.9 %branch_1_fun.1 = bf16[192,4096]{1,0:T(8,128)(2,1)S(1)} custom-call(s32[8,32]{1,0:T(8,128)} %get-tuple-element.58.vert, s32[2,32]{1,0:T(2,128)} %get-tuple-element.59.slash, s32[2,32]{1,0:T(2,128)} %get-tuple-element.60.counts, s32[2,16]{1,0:T(2,128)S(1)} %get-tuple-element.61.pack, s32[2,16]{1,0:T(2,128)S(1)} %get-tuple-element.62.row_pack, ...), custom_call_target="tpu_custom_call" | custom-call | tf_op jit(solution)/shard_map/cond/branch_1_fun/pallas_call | solution.py:402
  60.8 1.1 %copy.18 = bf16[192,4096]{1,0:T(8,128)(2,1)} copy(bf16[192,4096]{1,0:T(8,128)(2,1)S(1)} %get-tuple-element.78) | data formatting | bytes 3145728

commit v4 on v3

--- a/solution.py
+++ b/solution.py
@@ -17,6 +17,7 @@
 
 BIG = 1 << 30
 NEG = -1e30
+PACK, ROW_PACK, SLOT_AT, START, USED, LISTS, TABLE_ROWS = 0, 2, 4, 6, 7, 8, 12
 EXP2_SCALE = math.log2(math.e) / math.sqrt(HD)
 MESH = pl.DeviceIdType.MESH
 
@@ -93,27 +94,27 @@
     return (acc / total).astype(jnp.bfloat16)
 
 
-def key_positions(head, seq, blocks_dev, vert, slash, counts, kpos_v, kpos_s):
-    n_vert = counts[0, head]
-    n_slash = counts[1, head]
+def key_positions(h, heads, seq, blocks_dev, table, kpos_v, kpos_s):
+    n_vert = table[USED, h]
+    n_slash = table[USED, heads + h]
     lane = lax.broadcasted_iota(jnp.int32, (8, HD), 1)
     for k in range(NV // 2):
-        pos = jnp.where(lane < BLK, vert[2 * k, head], vert[2 * k + 1, head]) * BLK + lane % BLK
+        pos = jnp.where(lane < BLK, table[LISTS + h, 2 * k], table[LISTS + h, 2 * k + 1]) * BLK + lane % BLK
         used = jnp.where(lane < BLK, 2 * k, 2 * k + 1) < n_vert
         kpos_v[:, k * HD : (k + 1) * HD] = jnp.where(used, pos, BIG)
     row = lax.broadcasted_iota(jnp.int32, (blocks_dev, HD), 0)
     col = lax.broadcasted_iota(jnp.int32, (blocks_dev, HD), 1)
     first = (row % 2 == 0) == (col < BLK)
-    block = seq * blocks_dev + row - jnp.where(first, slash[0, head], slash[1, head])
+    block = seq * blocks_dev + row - jnp.where(first, table[USED, 2 * heads + h], table[USED, 3 * heads + h])
     dead = (block < 0) | (jnp.where(first, 0, 1) >= n_slash)
     for j in range(NV):
-        dead = dead | ((block == vert[j, head]) & (jnp.full_like(row, j) < n_vert))
+        dead = dead | ((block == table[LISTS + h, j]) & (jnp.full_like(row, j) < n_vert))
     kpos_s[...] = jnp.where(dead, BIG, block * BLK + col % BLK)
 
 
 def fused(
     nz, ny, ntp, slots, packed, row_packed,
-    vert, slash, counts, pack, row_pack, slot_at, starts, q_hbm, k_hbm, v_hbm, out,
+    table, q_hbm, k_hbm, v_hbm, out,
     q_ref, wk, wv, hk, hv, snd, got1k, got1v, mid, got2k, got2v, col, kv,
     obuf, obox, kpos_v, kpos_s,
     local_sem, halo_send, halo_recv, send1, recv1, send2, recv2, send3, recv3,
@@ -143,25 +144,25 @@
         local(1, v_hbm, wv.at[HALO:]),
         local(2, q_hbm, q_ref),
     ]
-    for c in copies:
+    for c in copies[:2]:
         c.start()
 
+    def far_first(n):
+        return sorted(range(1, n), key=lambda d: -min(d, n - d))
+
     barrier = pltpu.get_barrier_semaphore()
-
-    for d in range(1, ny):
-        peer = z * ny + lax.rem(y + d, ny)
-        pl.semaphore_signal(barrier, inc=1, device_id=(peer, tp), device_id_type=MESH)
-    for d in range(1, nz):
-        peer = lax.rem(z + d, nz) * ny + y
-        pl.semaphore_signal(barrier, inc=1, device_id=(peer, tp), device_id_type=MESH)
-    for d in range(1, ntp):
-        pl.semaphore_signal(
-            barrier, inc=1, device_id=(seq, lax.rem(tp + d, ntp)), device_id_type=MESH
-        )
+    for d in far_first(max(ny, nz)):
+        for peer in ((z * ny + lax.rem(y + d, ny)), (lax.rem(z + d, nz) * ny + y)):
+            pl.semaphore_signal(barrier, inc=1, device_id=(peer, tp), device_id_type=MESH)
 
     after, before = lax.rem(seq + 1, nseq), lax.rem(seq + nseq - 1, nseq)
     for peer in (after, before):
         pl.semaphore_signal(barrier, inc=1, device_id=(peer, tp), device_id_type=MESH)
+    for d in far_first(ntp):
+        pl.semaphore_signal(
+            barrier, inc=1, device_id=(seq, lax.rem(tp + d, ntp)), device_id_type=MESH
+        )
+    copies[2].start()
 
     kv[slots:] = jnp.zeros_like(kv[slots:])
     copies[0].wait()
@@ -173,7 +174,7 @@
 
         @pl.loop(0, packed)
         def _(k, side=side, n=n, piece=piece):
-            row = pack[side, k] * BLK + HALO
+            row = table[PACK + side, k] * BLK + HALO
             rows_k = wk[pl.ds(row, BLK), :]
             rows_v = wv[pl.ds(row, BLK), :]
             for c in range(n):
@@ -242,9 +243,6 @@
             device_id_type=MESH,
         )
 
-    def far_first(n):
-        return sorted(range(1, n), key=lambda d: -min(d, n - d))
-
     def each(axis, step):
         for d in far_first(max(ny, nz)):
             for side in (0, 1):
@@ -261,7 +259,7 @@
         for d in range(1, axes[side][0]):
             spread1(side, d).wait_recv()
         for k in range(row_packed):
-            mid[side, k] = got1[side][row_pack[side, k]]
+            mid[side, k] = got1[side][table[ROW_PACK + side, k]]
         for d in far_first(axes[side][1]):
             gather2(side, d).start()
     halo[1].start()
@@ -273,7 +271,7 @@
         for d in range(1, axes[side][1]):
             gather2(side, d).wait_recv()
         for i in range(half):
-            col[side, i] = got2[side][slot_at[side, i]]
+            col[side, i] = got2[side][table[SLOT_AT + side, i]]
         for d in far_first(axes[side][0]):
             gather1(0, side, d).start()
     each(0, lambda side, d: gather1(1, side, d).start())
@@ -330,13 +328,12 @@
         )
 
     def run_head(h, slot0):
-        head = tp * heads + h
-        key_positions(head, seq, blocks_dev, vert, slash, counts, kpos_v, kpos_s)
+        key_positions(h, heads, seq, blocks_dev, table, kpos_v, kpos_s)
         if isinstance(h, int):
             each(0, lambda side, d: gather1(0, side, d).wait_recv())
         refs = (
             q_ref, wk, wv, kv, kpos_v, kpos_s,
-            (slash[0, head], slash[1, head]), seq * tok,
+            (table[USED, 2 * heads + h], table[USED, 3 * heads + h]), seq * tok,
         )
         for j, step in enumerate(order):
             chip = lax.rem(x + step, nx)
@@ -354,7 +351,7 @@
 
     @pl.loop(1, heads)
     def _(h):
-        run_head(h, starts[h])
+        run_head(h, table[START, h])
 
     @pl.loop(0, heads)
     def _(h):
@@ -387,7 +384,7 @@
         each(0, lambda side, d: gather1(chunk, side, d).wait_send())
 
 
-def attend(nz, ny, ntp, slots, packed, row_packed, lists, tables, queries, keys, values):
+def attend(nz, ny, ntp, slots, packed, row_packed, table, queries, keys, values):
     tok, width = queries.shape
     heads = width // HD
     part = tok // ntp
@@ -402,7 +399,7 @@
     return pl.pallas_call(
         functools.partial(fused, nz, ny, ntp, slots, packed, row_packed),
         out_shape=jax.ShapeDtypeStruct((part, width * ntp), bf),
-        in_specs=[smem] * 7 + [hbm] * 3,
+        in_specs=[smem] + [hbm] * 3,
         out_specs=pl.BlockSpec(memory_space=pl.ANY),
         scratch_shapes=[
             pltpu.VMEM((tok, width), bf),
@@ -441,7 +438,7 @@
             has_side_effects=True,
             vmem_limit_bytes=60 * 2**20,
         ),
-    )(*lists, *tables, queries, keys, values)
+    )(table, queries, keys, values)
 
 
 FEW = 3
@@ -449,7 +446,7 @@
 FEW_SLOTS = 20
 
 
-def plan(nz, ny, heads, blocks_dev, vert, counts, vert_v, counts_v, pack, row_pack, slot_at, starts, few, wide, wide_n, listed):
+def plan(nz, ny, heads, blocks_dev, vert, slash, counts, vert_v, counts_v, table, few, wide, wide_n, listed):
     all_heads = vert.shape[1]
     seq, tp = lax.axis_index("seq"), lax.axis_index("tp")
     quad = NV // 2
@@ -494,69 +491,77 @@
     is_few = jnp.max(jnp.where((lane < all_heads) & over, 1, 0)) == 0
     few[0] = is_few.astype(jnp.int32)
 
-    @pl.loop(0, heads * NV)
-    def _(p):
+    for p in range(heads * NV):
         listed[p] = 0
-
     end = jnp.int32(1)
     for head in range(heads):
-        starts[head] = end
-        n = counts[0, tp * heads + head]
+        at = tp * heads + head
+        n = counts[0, at]
+        table[START, head] = end
+        table[USED, head] = n
+        table[USED, heads + head] = counts[1, at]
+        for j in range(NS):
+            table[USED, (2 + j) * heads + head] = slash[j, at]
+        table[LISTS + head, 0] = vert[0, at]
         for j in range(1, NV):
+            block = vert[j, at]
+            table[LISTS + head, j] = block
 
             @pl.when(j < n)
-            def _(j=j, head=head, end=end):
-                listed[end + j - 1] = vert[j, tp * heads + head]
+            def _(j=j, end=end, block=block):
+                listed[end + j - 1] = block
 
         end = end + n - 1
+    my_z = lax.div(seq, ny)
+    my_y = seq - my_z * ny
 
     def split(block):
         by = lax.div(block, blocks_dev)
         z = lax.div(by, ny)
         return by, z, by - z * ny
 
+    def place_at(side, half, i):
+        return side * quad + i if i < quad else NV + side * (half - quad) + i - quad
+
     def tables(slots, packed, row_packed):
         half = slots // 2
         sparse = packed == FEW
         for side in (0, 1):
-
-            def at(i, side=side):
-                return jnp.where(i < quad, side * quad + i, NV + side * (half - quad) + i - quad)
-
-            for k in range(packed):
-                pack[side, k] = 0
-            for k in range(row_packed):
-                row_pack[side, k] = 0
-
-            @pl.loop(0, half)
-            def _(i, side=side, at=at):
-                p = at(i)
-                owner, z, y = split(listed[p])
+            mine = my_z if side == 0 else my_y
+            if sparse:
+                for k in range(packed):
+                    table[PACK + side, k] = 0
+                for k in range(row_packed):
+                    table[ROW_PACK + side, k] = 0
+            owners, rows = [], []
+            for i in range(half):
+                p = place_at(side, half, i)
+                block = listed[p]
+                owner, z, y = split(block)
                 first, second = (y, z) if side == 0 else (z, y)
-                inside = listed[p] - owner * blocks_dev
-                my_second = lax.div(seq, ny) if side == 0 else lax.rem(seq, ny)
-                real = p < end
-
-                def count(o, c):
-                    other, oz, oy = split(listed[at(o)])
-                    same = (other == owner) & real
-                    same_row = ((oz if side == 0 else oy) == second) & real
-                    return c[0] + same.astype(jnp.int32), c[1] + same_row.astype(jnp.int32)
-
-                if sparse:
-                    place, row_place = lax.fori_loop(0, i, count, (jnp.int32(0), jnp.int32(0)))
-                else:
-                    place = row_place = i
-
-                @pl.when((owner == seq) & real)
-                def _():
-                    pack[side, place] = inside
-
-                @pl.when((second == my_second) & real)
-                def _():
-                    row_pack[side, row_place] = first * packed + place
-
-                slot_at[side, i] = second * row_packed + row_place
+                inside = block - owner * blocks_dev
+                if not sparse:
+                    table[PACK + side, i] = inside
+                    table[ROW_PACK + side, i] = first * packed + i
+                    table[SLOT_AT + side, i] = second * row_packed + i
+                    continue
+                real = (p < end).astype(jnp.int32)
+                place = row_place = jnp.int32(0)
+                for other, other_row in zip(owners, rows):
+                    place = place + (other == owner).astype(jnp.int32)
+                    row_place = row_place + (other_row == second).astype(jnp.int32)
+                owners.append(owner)
+                rows.append(second)
+                place, row_place = place * real, row_place * real
+                table[SLOT_AT + side, i] = second * row_packed + row_place
+
+                @pl.when((owner == seq) & (p < end))
+                def _(place=place, inside=inside, side=side):
+                    table[PACK + side, place] = inside
+
+                @pl.when((second == mine) & (p < end))
+                def _(place=place, row_place=row_place, first=first, side=side):
+                    table[ROW_PACK + side, row_place] = first * packed + place
 
     @pl.when(is_few)
     def _():
@@ -572,29 +577,30 @@
     heads = width // HD
     half = heads * NV // 2
     lists = (vertical.T, slash.T, counts.T)
-    table = jax.ShapeDtypeStruct((2, half), jnp.int32)
     smem = pl.BlockSpec(memory_space=pltpu.SMEM)
     vmem = pl.BlockSpec(memory_space=pltpu.VMEM)
-    *tables, few = pl.pallas_call(
+    table, few = pl.pallas_call(
         functools.partial(plan, nz, ny, heads, tok // BLK),
-        out_shape=(table,) * 3
-        + (jax.ShapeDtypeStruct((heads,), jnp.int32), jax.ShapeDtypeStruct((1,), jnp.int32)),
-        in_specs=[smem, smem, vmem, vmem],
-        out_specs=(smem,) * 5,
+        out_shape=(
+            jax.ShapeDtypeStruct((TABLE_ROWS, half), jnp.int32),
+            jax.ShapeDtypeStruct((1,), jnp.int32),
+        ),
+        in_specs=[smem, smem, smem, vmem, vmem],
+        out_specs=(smem, smem),
         scratch_shapes=[
             pltpu.VMEM((NV, HD), jnp.int32),
             pltpu.VMEM((NV, HD), jnp.int32),
             pltpu.SMEM((heads * NV,), jnp.int32),
         ],
-    )(lists[0], lists[2], lists[0], lists[2])
-
-    def sparse(tables, *args):
-        return attend(nz, ny, ntp, FEW_SLOTS, FEW, FEW_ROW, lists, tables, *args)
-
-    def dense(tables, *args):
-        return attend(nz, ny, ntp, heads * NV, half, half, lists, tables, *args)
-
-    return lax.cond(few[0] > 0, sparse, dense, tables, queries, keys, values)
+    )(*lists, lists[0], lists[2])
+
+    def sparse(*args):
+        return attend(nz, ny, ntp, FEW_SLOTS, FEW, FEW_ROW, *args)
+
+    def dense(*args):
+        return attend(nz, ny, ntp, heads * NV, half, half, *args)
+
+    return lax.cond(few[0] > 0, sparse, dense, table, queries, keys, values)
 
 
 def solution(mesh):

time: 62.2 us -> 61.4 us (0.987)
  Pallas kernels: 60 us -> 59.2 us
    pallas_call x1, Pallas kernels: 4.06 us -> 2.36 us  [per_device(): pl.pallas_call(functools.partial(plan, nz, ny, heads, tok // BLK), out_sh...]
    pallas_call x1, Pallas kernels: 55.9 us -> 56.8 us  [attend(): pl.pallas_call(functools.partial(fused, nz, ny, ntp, slots, packed, row_p...]
where the time goes in v4:
time: 61.4 us; the launch traced here: 61.2 us
  Pallas kernels  59.2 us (96%)
  local copies, waits for them, and re-layouts  1.15 us (2%)
  between operations  0.67 us (1%)
    pallas_call x1, Pallas kernels, attend(): pl.pallas_call(functools.partial(fused, nz, ny, ntp, slots, packed, row_p...  56.8 us
    pallas_call x1, Pallas kernels, per_device(): pl.pallas_call(functools.partial(plan, nz, ny, heads, tok // BLK), out_sh...  2.36 us

profile of v4, /device:TPU:1, one launch (start us, length us, event | category | flops | bytes accessed | tf_op | source)
XLA Modules:
  0.0 61.2 jit_solution(1593565507039816919)
XLA Ops:
  0.0 2.4 %shard_map.66 = (s32[12,16]{1,0:T(8,128)S(1)}, s32[1]{0:T(128)}) custom-call(s32[8,32]{1,0:T(8,128)} %bitcast.4, s32[2,32]{1,0:T(2,128)} %bitcast.8, s32[2,32]{1,0:T(2,128)} %bitcast.6, s32[8,32]{1,0:T(8,128)} %bitcast.5, s32[2,32]{1,0:T(2,128)} %bitcast.7), custom_call_target="tpu_custom_call" | custom-call | tf_op jit(solution)/shard_map/pallas_call | solution.py:582
  3.0 57.0 %conditional.1 = (bf16[192,4096]{1,0:T(8,128)(2,1)S(1)}) conditional(s32[]{:T(128)} %bitcast.3, (s32[12,16]{1,0:T(8,128)S(1)}, bf16[1536,512]{1,0:T(8,128)(2,1)}, bf16[1536,128]{1,0:T(8,128)(2,1)}, bf16[1536,128]{1,0:T(8,128)(2,1)}) %tuple.11, (s32[12,16]{1,0:T(8,128)S(1)}, bf16[1536,512]{1,0:T(8,128)(2,1)}, bf16[1536,128]{1,0:T(8,128)(2,1)}, ...), branch_computations={%region_0.0_spmd, %region_1.0_spmd} | conditional | bytes 8 | solution.py:603
  3.2 56.8 %branch_1_fun.1 = bf16[192,4096]{1,0:T(8,128)(2,1)S(1)} custom-call(s32[12,16]{1,0:T(8,128)S(1)} %get-tuple-element.28.table, bf16[1536,512]{1,0:T(8,128)(2,1)} %get-tuple-element.29.q_hbm, bf16[1536,128]{1,0:T(8,128)(2,1)} %get-tuple-element.30.k_hbm, bf16[1536,128]{1,0:T(8,128)(2,1)} %get-tuple-element.31.v_hbm), custom_call_target="tpu_custom_call" | custom-call | tf_op jit(solution)/shard_map/cond/branch_1_fun/pallas_call | solution.py:399
  60.1 1.1 %copy.12 = bf16[192,4096]{1,0:T(8,128)(2,1)} copy(bf16[192,4096]{1,0:T(8,128)(2,1)S(1)} %get-tuple-element.36) | data formatting | bytes 3145728
